TPU v7x, 512 devices: a whole 4x8x8 slice. The times are simulated.
512 devices in a mesh: fsdp: 32 (over z, x), tensor: 16 (over y, core).
Axes of the slice: x: 4, y: 8, z: 8, core: 2. Of those that a mesh axis runs over, the one named last changes fastest.
Arguments:
- gate_pre: bfloat16 [4096, 26624], P('fsdp', 'tensor'), may hold values from -6 to 6
- up_pre: bfloat16 [4096, 26624], P('fsdp', 'tensor'), may hold values from -6 to 6
- out_grad: bfloat16 [4096, 8192], P('fsdp', 'tensor'), may hold values from -6 to 6
- down_blocks: bfloat16 [96, 16, 128, 128], P('fsdp', 'tensor'), may hold values from -0.109375 to 0.109375
- block_rows: int32 [96, 16], P(None, 'tensor'), may hold values from 0 to 12, as said below
- block_cols: int32 [96, 16], P(None, 'tensor'), may hold values from 0 to 63
Outputs:
- output: bfloat16 [4096, 8192], P('fsdp', 'tensor')
- d_gate: bfloat16 [4096, 26624], P('fsdp', 'tensor')
- d_up: bfloat16 [4096, 26624], P('fsdp', 'tensor')
- grad_blocks: float32 [96, 16, 128, 128], P('fsdp', 'tensor')
Inputs may be any that keep to these rules, and one draw needn't show every extreme that they name: Within one rank t the pairs (block_rows[k, t], block_cols[k, t]) are distinct.
All inputs are finite; a program needn't handle non-finite values.
Results may differ from a plain program's by a relative error of at most 0.02.
Values may be sent and summed in bfloat16 or wider, within the bound.
No kernel may reach another device: no remote copies, remote signals or barrier semaphores. Data moves between devices by JAX's collectives and lax.ppermute only.
A program may use at most 64 MiB of HBM per device.

v0:
```python
import jax
import jax.numpy as jnp
from jax import lax
from jax.sharding import PartitionSpec as P

D = 8192


def forward_terms(summed, blocks, tile_rows, tile_columns, hidden_tiles):
    chosen = jnp.take(hidden_tiles, tile_rows, axis=1)
    contrib = jnp.einsum("tbi,bij->tbj", chosen, blocks, preferred_element_type=jnp.float32)
    return summed.at[:, tile_columns].add(contrib)


def backward_terms(backed, blocks, tile_rows, tile_columns, grad_tiles):
    chosen = jnp.take(grad_tiles, tile_columns, axis=1)
    contrib = jnp.einsum("tbj,bij->tbi", chosen, blocks, preferred_element_type=jnp.float32)
    return backed.at[:, tile_rows].add(contrib)


def block_grads(hidden_tiles, grad_tiles, tile_rows, tile_columns):
    left_tiles = jnp.take(hidden_tiles, tile_rows, axis=1)
    right_tiles = jnp.take(grad_tiles, tile_columns, axis=1)
    return jnp.einsum("tbi,tbj->bij", left_tiles, right_tiles, preferred_element_type=jnp.float32)


def shards(gate_pre, up_pre, out_grad, down_blocks, block_rows, block_cols):
    tokens_here = gate_pre.shape[0]
    block_edge = down_blocks.shape[-1]
    hidden_count = gate_pre.shape[1] // block_edge
    width_count = D // block_edge
    gate_full = gate_pre.astype(jnp.float32)
    up_full = up_pre.astype(jnp.float32)
    sigma = jax.nn.sigmoid(gate_full)
    hidden = (gate_full * sigma * up_full).astype(jnp.bfloat16)
    hidden_tiles = hidden.reshape(tokens_here, hidden_count, block_edge)
    tile_rows = block_rows[:, 0]
    tile_columns = block_cols[:, 0]
    group_count = tile_rows.shape[0]
    whole_grad = lax.all_gather(out_grad, "tensor", axis=1, tiled=True)
    grad_tiles = whole_grad.reshape(tokens_here, width_count, block_edge)
    empty_out = jnp.zeros((tokens_here, width_count, block_edge), jnp.float32)
    empty_back = jnp.zeros((tokens_here, hidden_count, block_edge), jnp.float32)
    gathered = lax.all_gather(down_blocks, "fsdp", axis=0, tiled=True)[:, 0]
    summed = forward_terms(empty_out, gathered, tile_rows, tile_columns, hidden_tiles)
    backed = backward_terms(empty_back, gathered, tile_rows, tile_columns, grad_tiles)
    partial_out = summed.reshape(tokens_here, D)
    output = lax.psum_scatter(
        partial_out.astype(jnp.bfloat16), "tensor", scatter_dimension=1, tiled=True
    )
    grad_hidden = backed.reshape(tokens_here, hidden_count * block_edge)
    d_gate = (grad_hidden * up_full * sigma * (1.0 + gate_full * (1.0 - sigma))).astype(
        jnp.bfloat16
    )
    d_up = (grad_hidden * gate_full * sigma).astype(jnp.bfloat16)
    owners = lax.axis_size("fsdp")
    owned = group_count // owners
    local_terms = block_grads(hidden_tiles, grad_tiles, tile_rows, tile_columns).astype(
        jnp.bfloat16
    )
    local_terms = local_terms.reshape(owners, owned, 1, block_edge, block_edge)
    arrived = lax.all_to_all(local_terms, "fsdp", split_axis=0, concat_axis=0, tiled=True)
    grad_blocks = jnp.sum(arrived, axis=0, dtype=jnp.float32)
    return (output, d_gate, d_up, grad_blocks)


def solution(mesh):
    in_specs = (
        P("fsdp", "tensor"),
        P("fsdp", "tensor"),
        P("fsdp", "tensor"),
        P("fsdp", "tensor", None, None),
        P(None, "tensor"),
        P(None, "tensor"),
    )
    out_specs = (
        P("fsdp", "tensor"),
        P("fsdp", "tensor"),
        P("fsdp", "tensor"),
        P("fsdp", "tensor", None, None),
    )
    return jax.shard_map(shards, mesh=mesh, in_specs=in_specs, out_specs=out_specs, check_vma=False)
```

profile of v0, /device:TPU:56, one launch (start us, length us, event | category | flops | bytes accessed | tf_op | source)
XLA Modules:
  0.0 287.9 jit_solution(14410198306093952574)
XLA Ops:
  7.2 1.7 copy.38
  8.9 0.0 all-gather.3.cloned.1.call-start
  8.9 0.7 all-gather.3.cloned.1.call-update
  9.7 1.3 copy.34
  10.9 1.3 copy.35
  12.2 0.7 compare_select_fusion
  12.9 0.7 compare_select_fusion.1
  13.5 0.7 fusion.25
  14.2 0.7 compare_and_fusion
  14.9 40.9 %all-gather.5.cloned.1.call-done = bf16[128,8192]{0,1:T(8,128)(2,1)} async-done(((bf16[128,512]{0,1:T(8,128)(2,1)}), bf16[128,8192]{0,1:T(8,128)(2,1)}) %all-gather.5.cloned.1.call-update) | async-done | bytes 2097168 | tf_op jit(solution)/shard_map/all_gather | solution.py:40
  55.7 3.2 %copy.39 = bf16[128,64,128]{2,0,1:T(8,128)(2,1)S(1)} copy(bf16[128,64,128]{0,2,1:T(8,128)(2,1)} %bitcast.43) | data formatting | bytes 4194304 | tf_op jit(solution)/shard_map/reshape | solution.py:41
  58.9 2.8 gather_fusion.1
  61.7 83.1 %all-gather.3.cloned.1.call-done = bf16[96,1,128,128]{3,2,1,0:T(8,128)(2,1)} async-done(((bf16[3,1,128,128]{3,2,1,0:T(8,128)(2,1)}), bf16[96,1,128,128]{3,2,1,0:T(8,128)(2,1)}) %all-gather.3.cloned.1.call-update) | async-done | bytes 3145744 | tf_op jit(solution)/shard_map/all_gather | solution.py:44
  144.8 7.8 %fusion.2 = f32[96,128,128]{2,1,0:T(8,128)} fusion(bf16[96,1,128,128]{3,2,1,0:T(8,128)(2,1)} %all-gather.3.cloned.1.call-done, bf16[96,128,128]{2,1,0:T(8,128)(2,1)} %gather_fusion.1, pred[96]{0:T(512)(128)(4,1)S(1)} %get-tuple-element.21), kind=kOutput, calls=%fused_computation.7 | convolution fusion | flops 404226048 | bytes 12583008 | tf_op jit(solution)/shard_map/tbj,bij->tbi/dot_general | solution.py:17
  152.7 0.1 broadcast_in_dim.27
  152.7 12.9 %scatter_fusion.1 = f32[128,13,128]{2,0,1:T(8,128)S(1)} fusion(f32[128,13,128]{2,0,1:T(8,128)S(1)} %broadcast_in_dim.27, s32[96]{0:T(128)S(1)} %fusion.25, f32[96,128,128]{2,1,0:T(8,128)} %fusion.2), kind=kCustom, calls=%fused_computation.3 | custom fusion | flops 1572864 | bytes 18874752 | tf_op jit(solution)/shard_map/scatter-add | solution.py:18
  165.7 0.3 copy.40
  166.0 1.4 fusion.23
  167.4 0.3 copy.36
  167.7 2.7 gather_fusion
  170.4 5.9 %fusion.9 = bf16[96,128,128]{2,1,0:T(8,128)(2,1)} fusion(bf16[96,128,128]{2,1,0:T(8,128)(2,1)} %gather_fusion, pred[96]{0:T(512)(128)(4,1)S(1)} %get-tuple-element.22, bf16[96,128,128]{2,1,0:T(8,128)(2,1)} %gather_fusion.1, pred[96]{0:T(512)(128)(4,1)S(1)} %get-tuple-element.21), kind=kOutput, calls=%fused_computation.16 | convolution fusion | flops 407371776 | bytes 9437376 | tf_op jit(solution)/shard_map/tbi,tbj->bij/dot_general | solution.py:24
  176.3 5.2 %all-to-all-start = ((bf16[32,3,1,128,128]{4,3,1,2,0:T(8,128)(2,1)}), bf16[32,3,1,128,128]{4,3,1,2,0:T(8,128)(2,1)S(1)}, u32[]{:S(2)}, u32[]{:S(2)}) async-start(bf16[32,3,1,128,128]{4,3,1,2,0:T(8,128)(2,1)} %bitcast.42), calls=%async_computation.1 | async-start | bytes 6291456 | tf_op jit(solution)/shard_map/all_to_all | solution.py:62
  181.5 6.5 %fusion.5 = f32[96,128,128]{2,1,0:T(8,128)} fusion(bf16[96,1,128,128]{3,2,1,0:T(8,128)(2,1)} %all-gather.3.cloned.1.call-done, bf16[96,128,128]{2,1,0:T(8,128)(2,1)} %gather_fusion, pred[96]{0:T(512)(128)(4,1)S(1)} %get-tuple-element.22), kind=kOutput, calls=%fused_computation.10 | convolution fusion | flops 404226048 | bytes 12583008 | tf_op jit(solution)/shard_map/tbi,bij->tbj/dot_general | solution.py:11
  188.0 2.5 broadcast_in_dim.26
  190.5 20.1 %scatter_fusion = f32[128,64,128]{2,0,1:T(8,128)} fusion(f32[128,64,128]{2,0,1:T(8,128)} %broadcast_in_dim.26, s32[96]{0:T(128)S(1)} %fusion.24, f32[96,128,128]{2,1,0:T(8,128)} %fusion.5), kind=kCustom, calls=%fused_computation.2 | custom fusion | flops 1572864 | bytes 18874752 | tf_op jit(solution)/shard_map/scatter-add | solution.py:12
  210.6 3.9 %convert_element_type.30 = bf16[128,64,128]{2,0,1:T(8,128)(2,1)} convert(f32[128,64,128]{2,0,1:T(8,128)} %scatter_fusion) | non-fusion elementwise | flops 1048576 | bytes 6291456 | tf_op jit(solution)/shard_map/convert_element_type | solution.py:49
  214.5 4.1 %copy.37 = bf16[128,64,128]{0,2,1:T(8,128)(2,1)} copy(bf16[128,64,128]{2,0,1:T(8,128)(2,1)} %convert_element_type.30) | data formatting | bytes 4194304 | tf_op jit(solution)/shard_map/convert_element_type | solution.py:49
  218.6 2.0 copy.44
  220.6 2.0 copy.45
  222.5 56.0 %reduce-scatter.2.cloned.1.call-done = bf16[128,512]{0,1:T(8,128)(2,1)} async-done(((bf16[128,8192]{0,1:T(8,128)(2,1)}), bf16[128,512]{0,1:T(8,128)(2,1)}) %reduce-scatter.2.cloned.1.call-update) | async-done | bytes 131088 | tf_op jit(solution)/shard_map/reduce_scatter | solution.py:48
  278.5 1.7 copy.43
  280.1 1.2 convert_reduce_fusion
  (10 shorter events, 0.1 us)
Async XLA Ops:
  7.2 48.6 %all-gather.5.cloned.1.call-start = ((), (), s32[]{:S(2)}) async-start(), calls=%async_computation.4 | async-start | bytes 2228224 | tf_op jit(solution)/shard_map/all_gather | solution.py:40
  8.9 135.9 %all-gather.3.cloned.1.call-start = ((), (), s32[]{:S(2)}) async-start(), calls=%async_computation.2 | async-start | bytes 3244032 | tf_op jit(solution)/shard_map/all_gather | solution.py:44
  176.3 5.2 %copy-start = (s32[96,1]{0,1:T(1,128)S(1)}, s32[96,1]{0,1:T(1,128)}, u32[]{:S(2)}) copy-start(s32[96,1]{0,1:T(1,128)} %param.15) | copy-start | bytes 1156
  176.3 103.9 %all-to-all-start = ((bf16[32,3,1,128,128]{4,3,1,2,0:T(8,128)(2,1)}), bf16[32,3,1,128,128]{4,3,1,2,0:T(8,128)(2,1)S(1)}, u32[]{:S(2)}, u32[]{:S(2)}) async-start(bf16[32,3,1,128,128]{4,3,1,2,0:T(8,128)(2,1)} %bitcast.42), calls=%async_computation.1 | async-start | bytes 6291456 | tf_op jit(solution)/shard_map/all_to_all | solution.py:62
  181.5 97.0 %reduce-scatter.2.cloned.1.call-start = ((), (), s32[]{:S(2)}) async-start(), calls=%async_computation.3 | async-start | bytes 2228224 | tf_op jit(solution)/shard_map/reduce_scatter | solution.py:48
Sparse Core Ops, SparseCore 0:
  10.7 44.9 all-gather.4
  58.9 85.8 all-gather.2
  218.7 59.7 reduce-scatter.1
where the time goes:
time: 293 us; the launch traced here: 288 us
  waiting for transfers between devices  181 us (62%)
  other arithmetic  42.3 us (14%)
  local copies, waits for them, and re-layouts  25.7 us (9%)
  matrix products  20.3 us (7%)
  between operations  13.8 us (5%)
  starting transfers between devices  5.31 us (2%)
    all_gather x1, waiting for transfers between devices, shards(): gathered = lax.all_gather(down_blocks, 'fsdp', axis=0, tiled=True)[:, 0]  83.1 us
    reduce_scatter x1, waiting for transfers between devices, shards(): lax.psum_scatter(partial_out.astype(jnp.bfloat16), 'tensor', scatter_dime...  56 us
    all_gather x1, waiting for transfers between devices, shards(): whole_grad = lax.all_gather(out_grad, 'tensor', axis=1, tiled=True)  40.9 us
    scatter-add x1, other arithmetic, forward_terms(): return summed.at[:, tile_columns].add(contrib)  20.1 us
    scatter-add x1, other arithmetic, backward_terms(): return backed.at[:, tile_rows].add(contrib)  12.9 us
    unnamed x8, local copies, waits for them, and re-layouts  9.8 us
    dot_general x1, matrix products, backward_terms(): jnp.einsum('tbj,bij->tbi', chosen, blocks, preferred_element_type=jnp.flo...  7.84 us
    dot_general x1, matrix products, forward_terms(): jnp.einsum('tbi,bij->tbj', chosen, blocks, preferred_element_type=jnp.flo...  6.49 us
  transfers between devices with their start and end apart: 4, of which 3 were waited for; matrix products, arithmetic and copies ran while one was open for 19% of the time, Pallas kernels for 0%

commit v1 on v0

v1 whole, which is shorter than its diff:
```python
import functools

import jax
import jax.numpy as jnp
from jax import lax
from jax.experimental import pallas as pl
from jax.experimental.pallas import tpu as pltpu
from jax.sharding import PartitionSpec as P

BLK = 128
HID_TILES = 13
WIDTH_TILES = 64
GROUP_BLOCKS = 96
OWNED = 3
FAR = 2
NX, NY, NZ = 4, 8, 8
STEP = 8
VMEM_BYTES = 48 * 1024 * 1024

SMEM = pl.BlockSpec(memory_space=pltpu.SMEM)
VMEM = pl.BlockSpec(memory_space=pltpu.VMEM)


def x_shift(step):
    return [(z * NX + x, z * NX + (x + step) % NX) for z in range(NZ) for x in range(NX)]


CORE_SWAP = [(t, t ^ 1) for t in range(2 * NY)]
Z_GROUPS = [[z * NX + x for z in range(NZ)] for x in range(NX)]
Y_GROUPS = [[y * 2 + c for y in range(NY)] for c in range(2)]


def call(kernel, outs, ins, scratch=(), flops=0, moved=0):
    return pl.pallas_call(
        kernel,
        out_shape=outs,
        in_specs=[SMEM if a.dtype == jnp.int32 else VMEM for a in ins],
        out_specs=jax.tree.map(lambda _: VMEM, outs),
        scratch_shapes=list(scratch),
        compiler_params=pltpu.CompilerParams(vmem_limit_bytes=VMEM_BYTES),
        cost_estimate=pl.CostEstimate(flops=flops, bytes_accessed=moved, transcendentals=0),
    )(*ins)


def tiles(n, dtype=jnp.bfloat16):
    return jax.ShapeDtypeStruct((n, BLK, BLK), dtype)


def block_of(z, x, place):
    return (z * NX + x) * OWNED + place


def far_at(a, i, me_x, sign):
    return block_of(i // FAR, lax.rem(me_x + sign * a + NX, NX), lax.rem(i, FAR))


def near_at(i, me_x, sign):
    return block_of(i // NX, lax.rem(me_x + sign * lax.rem(i, NX) + NX, NX), FAR)


def each_block(parts, me_x, sign, visit):
    for a, ref in enumerate(parts):
        def some(g, carry, a=a, ref=ref):
            entries = [g * STEP + j for j in range(STEP)]
            visit(ref, [(i, far_at(a, i, me_x, sign) if a < NX else near_at(i, me_x, sign)) for i in entries])
            return carry
        lax.fori_loop(0, ref.shape[0] // STEP, some, 0)


def hidden_kernel(gate_ref, up_ref, hid_ref, hid_t_ref):
    for r in range(HID_TILES):
        here = slice(r * BLK, (r + 1) * BLK)
        gate = gate_ref[:, here].astype(jnp.float32)
        hidden = gate * jax.nn.sigmoid(gate) * up_ref[:, here].astype(jnp.float32)
        hid_ref[r] = hidden.astype(jnp.bfloat16)
        hid_t_ref[r] = hidden.T.astype(jnp.bfloat16)


def terms_kernel(rows_ref, cols_ref, me_ref, hid_t_ref, grad_ref, *out_refs):
    def visit(ref, entries):
        for i, k in entries:
            ref[i] = jnp.dot(
                hid_t_ref[rows_ref[k]], grad_ref[cols_ref[k]], preferred_element_type=jnp.float32
            ).astype(jnp.bfloat16)
    each_block(out_refs, me_ref[0], 1, visit)


def forward_kernel(rows_ref, cols_ref, me_ref, hid_ref, *refs):
    parts, (out_ref, total) = refs[:NX + 1], refs[NX + 1:]
    total[...] = jnp.zeros_like(total)

    def visit(ref, entries):
        found = [
            (cols_ref[k], jnp.dot(hid_ref[rows_ref[k]], ref[i], preferred_element_type=jnp.float32)) for i, k in entries
        ]
        for c, value in found:
            total[c] += value
    each_block(parts, me_ref[0], -1, visit)

    def put(y, carry):
        for j in range(8):
            out_ref[y * 8 + j] = total[y * 8 + j].astype(jnp.bfloat16)
        return carry
    lax.fori_loop(0, NY, put, 0)


def backward_kernel(rows_ref, cols_ref, me_ref, grad_ref, gate_ref, up_ref, *refs):
    parts, (d_gate_ref, d_up_ref, total) = refs[:NX + 1], refs[NX + 1:]
    total[...] = jnp.zeros_like(total)

    def visit(ref, entries):
        found = [
            (rows_ref[k], lax.dot_general(
                grad_ref[cols_ref[k]], ref[i], (((1,), (1,)), ((), ())), preferred_element_type=jnp.float32
            )) for i, k in entries
        ]
        for r, value in found:
            total[r] += value
    each_block(parts, me_ref[0], -1, visit)
    for r in range(HID_TILES):
        here = slice(r * BLK, (r + 1) * BLK)
        gate = gate_ref[:, here].astype(jnp.float32)
        up = up_ref[:, here].astype(jnp.float32)
        sigma = jax.nn.sigmoid(gate)
        back = total[r]
        d_gate_ref[:, here] = (back * up * sigma * (1.0 + gate * (1.0 - sigma))).astype(jnp.bfloat16)
        d_up_ref[:, here] = (back * gate * sigma).astype(jnp.bfloat16)


def near_sum_kernel(arrived_ref, *out_refs):
    for b, out_ref in enumerate(out_refs):
        total = arrived_ref[b].astype(jnp.float32)
        for z in range(1, NZ):
            total += arrived_ref[z * NX + b].astype(jnp.float32)
        out_ref[0] = total.astype(jnp.bfloat16)


def block_sum_kernel(far_ref, *refs):
    near_refs, out_ref = refs[:NX], refs[NX]
    for j in range(FAR):
        total = far_ref[j].astype(jnp.float32)
        for z in range(1, NZ):
            total += far_ref[z * FAR + j].astype(jnp.float32)
        out_ref[j] = total
    total = near_refs[0][0].astype(jnp.float32)
    for ref in near_refs[1:]:
        total += ref[0].astype(jnp.float32)
    out_ref[FAR] = total


def z_exchange(a):
    return lax.all_to_all(a, "fsdp", 0, 0, tiled=True, axis_index_groups=Z_GROUPS)


def to_all(a):
    return jnp.broadcast_to(a[None], (NZ, *a.shape)).reshape(NZ * a.shape[0], BLK, BLK)


def shards(gate_pre, up_pre, out_grad, down_blocks, block_rows, block_cols):
    rows, cols = block_rows[:, 0], block_cols[:, 0]
    me = jnp.stack([lax.rem(lax.axis_index("fsdp"), NX), lax.rem(lax.axis_index("tensor"), 2)]).astype(jnp.int32)
    macs = GROUP_BLOCKS * BLK**3
    blocks = down_blocks.reshape(OWNED, BLK, BLK)

    with jax.named_scope("gather_out_grad"):
        grad_tiles = out_grad.reshape(BLK, 4, BLK).transpose(1, 0, 2)
        grad_tiles, blocks = lax.optimization_barrier((grad_tiles, blocks))
        grad_tiles = lax.all_gather(grad_tiles, "tensor", axis=0, tiled=True)
    with jax.named_scope("gather_blocks"):
        far = z_exchange(to_all(blocks[:FAR]))
        near = blocks[FAR:]
        near = jnp.concatenate([near] + [lax.ppermute(near, "fsdp", x_shift(s)) for s in range(1, NX)], axis=0)
        near = z_exchange(to_all(near))
        parts = [far] + [lax.ppermute(far, "fsdp", x_shift(s)) for s in range(1, NX)] + [near]
    with jax.named_scope("hidden"):
        hid, hid_t = call(hidden_kernel, (tiles(HID_TILES), tiles(HID_TILES)), (gate_pre, up_pre), flops=10**9, moved=4 * 10**6)
    with jax.named_scope("terms"):
        outs = tuple(tiles(NZ * FAR) for _ in range(NX)) + (tiles(NZ * NX),)
        terms = call(terms_kernel, outs, (rows, cols, me, hid_t, grad_tiles), flops=8 * macs, moved=6 * 10**6)
        terms, hid = lax.optimization_barrier((terms, hid))
    with jax.named_scope("sum_terms_first"):
        far_terms = [terms[0]] + [lax.ppermute(terms[s], "fsdp", x_shift(s)) for s in range(1, NX)]
        near_terms = z_exchange(terms[NX])
    with jax.named_scope("forward"):
        summed = call(
            forward_kernel, tiles(64), (rows, cols, me, hid, *parts),
            scratch=[pltpu.VMEM((WIDTH_TILES, BLK, BLK), jnp.float32)], flops=8 * macs, moved=6 * 10**6,
        )
    with jax.named_scope("sum_output"):
        output = lax.psum_scatter(summed, "tensor", scatter_dimension=0, tiled=True)
        output = output.transpose(1, 0, 2).reshape(BLK, 4 * BLK)
    with jax.named_scope("backward"):
        wide = jax.ShapeDtypeStruct(gate_pre.shape, jnp.bfloat16)
        d_gate, d_up = call(
            backward_kernel, (wide, wide), (rows, cols, me, grad_tiles, gate_pre, up_pre, *parts),
            scratch=[pltpu.VMEM((HID_TILES, BLK, BLK), jnp.float32)], flops=8 * macs, moved=8 * 10**6,
        )
    with jax.named_scope("sum_terms_second"):
        far_terms = functools.reduce(jnp.add, [a.astype(jnp.float32) for a in far_terms]).astype(jnp.bfloat16)
        far_terms = z_exchange(far_terms)
        near_terms = call(near_sum_kernel, tuple(tiles(1) for _ in range(NX)), (near_terms,), moved=10**6)
        near_terms = [near_terms[0]] + [lax.ppermute(near_terms[s], "fsdp", x_shift(s)) for s in range(1, NX)]
        grad_blocks = call(block_sum_kernel, tiles(OWNED, jnp.float32), (far_terms, *near_terms), moved=10**6)
        grad_blocks = grad_blocks.reshape(OWNED, 1, BLK, BLK)
    return (output, d_gate, d_up, grad_blocks)


def solution(mesh):
    both = P("fsdp", "tensor")
    blocks = P("fsdp", "tensor", None, None)
    index = P(None, "tensor")
    return jax.shard_map(
        shards, mesh=mesh, in_specs=(both, both, both, blocks, index, index),
        out_specs=(both, both, both, blocks), check_vma=False,
    )
```

time: 293 us -> 160 us (0.55); the launches traced: 288 us -> 159 us
  waiting for transfers between devices: 181 us -> 32.9 us
  starting transfers between devices: 5.31 us -> 72.7 us
  other arithmetic: 42.3 us -> 1.22 us
  matrix products: 20.3 us -> 0 us
  Pallas kernels: 0 us -> 16.4 us
  local copies, waits for them, and re-layouts: 25.7 us -> 21 us
    all_gather x2 -> x1, waiting for transfers between devices: 124 us -> 0.01 us  [shards(): grad_tiles = lax.all_gather(grad_tiles, 'tensor', axis=0, tiled=True)]
    reduce_scatter x1, waiting for transfers between devices: 56 us -> 0.01 us  [shards(): output = lax.psum_scatter(summed, 'tensor', scatter_dimension=0, tiled=True)]
    ppermute x0 -> x12, starting transfers between devices: none -> 44.1 us  [the longest x3 11.4 us: shards(): lax.ppermute(near, 'fsdp', x_shift(s))]
    scatter-add x2 -> x0, other arithmetic: 33 us -> none  [the longest x1 20.1 us: forward_terms(): return summed.at[:, tile_columns].add(contrib)]
    ppermute x0 -> x12, waiting for transfers between devices: none -> 30 us  [the longest x3 18.9 us: shards(): lax.ppermute(terms[s], 'fsdp', x_shift(s))]
    all_to_all x1 -> x4, starting transfers between devices: 5.19 us -> 28.6 us  [z_exchange(): lax.all_to_all(a, 'fsdp', 0, 0, tiled=True, axis_index_groups=Z_GROUPS)]
    dot_general x3 -> x0, matrix products: 20.3 us -> none  [the longest x1 7.84 us: backward_terms(): jnp.einsum('tbj,bij->tbi', chosen, blocks, preferred_element_type=jnp.flo...]
    pallas_call x0 -> x6, Pallas kernels: none -> 16.4 us  [call(): pl.pallas_call(kernel, out_shape=outs, in_specs=[SMEM if a.dtype == jnp.i...]
  transfers between devices with their start and end apart: 4 -> 18, of which waited for: 3 -> 7; matrix products, arithmetic and copies ran while one was open for 19% -> 3% of each run, Pallas kernels for 0% -> 7%
where the time goes in v1:
time: 160 us; the launch traced here: 159 us
  starting transfers between devices  72.7 us (45%)
  waiting for transfers between devices  32.9 us (21%)
  local copies, waits for them, and re-layouts  21 us (13%)
  Pallas kernels  16.4 us (10%)
  between operations  14.3 us (9%)
    all_to_all x4, starting transfers between devices, z_exchange(): lax.all_to_all(a, 'fsdp', 0, 0, tiled=True, axis_index_groups=Z_GROUPS)  28.6 us
    ppermute x3, waiting for transfers between devices, shards(): lax.ppermute(terms[s], 'fsdp', x_shift(s))  18.9 us
    pallas_call x6, Pallas kernels, call(): pl.pallas_call(kernel, out_shape=outs, in_specs=[SMEM if a.dtype == jnp.i...  16.4 us
    unnamed x42, local copies, waits for them, and re-layouts  15.5 us
    ppermute x3, starting transfers between devices, shards(): lax.ppermute(near, 'fsdp', x_shift(s))  11.4 us
    ppermute x3, starting transfers between devices, shards(): lax.ppermute(terms[s], 'fsdp', x_shift(s))  11.4 us
    ppermute x3, starting transfers between devices, shards(): lax.ppermute(near_terms[s], 'fsdp', x_shift(s))  10.8 us
    ppermute x3, starting transfers between devices, shards(): lax.ppermute(far, 'fsdp', x_shift(s))  10.6 us
  transfers between devices with their start and end apart: 18, of which 7 were waited for; matrix products, arithmetic and copies ran while one was open for 3% of the time, Pallas kernels for 7%

profile of v1, /device:TPU:56, one launch (start us, length us, event | category | flops | bytes accessed | tf_op | source)
XLA Modules:
  0.0 158.6 jit_solution(14167140422966316751)
XLA Ops:
  10.8 10.4 %all-to-all-start = ((bf16[16,128,128]{2,1,0:T(8,128)(2,1)}), bf16[16,128,128]{2,1,0:T(8,128)(2,1)S(1)}, u32[]{:S(2)}, u32[]{:S(2)}) async-start(bf16[16,128,128]{2,1,0:T(8,128)(2,1)} %bitcast.7), calls=%async_computation | async-start | bytes 1048576 | tf_op jit(solution)/shard_map/gather_blocks/all_to_all | solution.py:152
  22.0 3.4 %collective-permute-start.3 = (bf16[1,128,128]{2,1,0:T(8,128)(2,1)S(1)}, bf16[1,128,128]{2,1,0:T(8,128)(2,1)S(1)}, u32[]{:S(2)}, u32[]{:S(2)}) collective-permute-start(bf16[1,128,128]{2,1,0:T(8,128)(2,1)S(1)} %slice.7), channel_id=1, source_target_pairs={{0,16},{16,32},{32,48},{48,0},{64,80},{80,96},{96,112},{112,64},{1... | collective-permute-start | bytes 98312 | tf_op jit(solution)/shard_map/gather_blocks/ppermute | solution.py:172
  25.4 4.6 %collective-permute-start.4 = (bf16[1,128,128]{2,1,0:T(8,128)(2,1)S(1)}, bf16[1,128,128]{2,1,0:T(8,128)(2,1)S(1)}, u32[]{:S(2)}, u32[]{:S(2)}) collective-permute-start(bf16[1,128,128]{2,1,0:T(8,128)(2,1)S(1)} %slice.7), channel_id=1, source_target_pairs={{0,32},{16,48},{32,0},{48,16},{64,96},{80,112},{96,64},{112,80},{1... | collective-permute-start | bytes 98312 | tf_op jit(solution)/shard_map/gather_blocks/ppermute | solution.py:172
  30.1 3.3 %collective-permute-start.5 = (bf16[1,128,128]{2,1,0:T(8,128)(2,1)S(1)}, bf16[1,128,128]{2,1,0:T(8,128)(2,1)S(1)}, u32[]{:S(2)}, u32[]{:S(2)}) collective-permute-start(bf16[1,128,128]{2,1,0:T(8,128)(2,1)S(1)} %slice.7), channel_id=1, source_target_pairs={{0,48},{16,0},{32,16},{48,32},{64,112},{80,64},{96,80},{112,96},{1... | collective-permute-start | bytes 98312 | tf_op jit(solution)/shard_map/gather_blocks/ppermute | solution.py:172
  33.4 2.4 %collective-permute-done.5 = bf16[1,128,128]{2,1,0:T(8,128)(2,1)S(1)} collective-permute-done((bf16[1,128,128]{2,1,0:T(8,128)(2,1)S(1)}, bf16[1,128,128]{2,1,0:T(8,128)(2,1)S(1)}, u32[]{:S(2)}, u32[]{:S(2)}) %collective-permute-start.5) | collective-permute-done | bytes 32800 | tf_op jit(solution)/shard_map/gather_blocks/ppermute | solution.py:172
  35.9 2.9 %all-to-all-done.refs_0_ = bf16[16,128,128]{2,1,0:T(8,128)(2,1)S(1)} async-done(((bf16[16,128,128]{2,1,0:T(8,128)(2,1)}), bf16[16,128,128]{2,1,0:T(8,128)(2,1)S(1)}, u32[]{:S(2)}, u32[]{:S(2)}) %all-to-all-start) | async-done | bytes 524320 | tf_op jit(solution)/shard_map/gather_blocks/all_to_all | solution.py:152
  38.7 1.2 broadcast_in_dim.5
  39.9 4.4 %all-to-all-start.1 = ((bf16[32,128,128]{2,1,0:T(8,128)(2,1)}), bf16[32,128,128]{2,1,0:T(8,128)(2,1)S(1)}, u32[]{:S(2)}, u32[]{:S(2)}) async-start(bf16[32,128,128]{2,1,0:T(8,128)(2,1)} %bitcast.8), calls=%async_computation.1 | async-start | bytes 2097152 | tf_op jit(solution)/shard_map/gather_blocks/all_to_all | solution.py:152
  44.4 2.6 %collective-permute-start = (bf16[16,128,128]{2,1,0:T(8,128)(2,1)S(1)}, bf16[16,128,128]{2,1,0:T(8,128)(2,1)S(1)}, u32[]{:S(2)}, u32[]{:S(2)}) collective-permute-start(bf16[16,128,128]{2,1,0:T(8,128)(2,1)S(1)} %all-to-all-done.refs_0_), channel_id=1, source_target_pairs={{0,16},{16,32},{32,48},{48,0},{64,80},{80,96},{96,112},{112,64},{1... | collective-permute-start | bytes 1572872 | tf_op jit(solution)/shard_map/gather_blocks/ppermute | solution.py:174
  47.0 5.3 %collective-permute-start.1 = (bf16[16,128,128]{2,1,0:T(8,128)(2,1)S(1)}, bf16[16,128,128]{2,1,0:T(8,128)(2,1)S(1)}, u32[]{:S(2)}, u32[]{:S(2)}) collective-permute-start(bf16[16,128,128]{2,1,0:T(8,128)(2,1)S(1)} %all-to-all-done.refs_0_), channel_id=1, source_target_pairs={{0,32},{16,48},{32,0},{48,16},{64,96},{80,112},{96,64},{112,80},{1... | collective-permute-start | bytes 1572872 | tf_op jit(solution)/shard_map/gather_blocks/ppermute | solution.py:174
  52.3 2.7 %collective-permute-start.2 = (bf16[16,128,128]{2,1,0:T(8,128)(2,1)S(1)}, bf16[16,128,128]{2,1,0:T(8,128)(2,1)}, u32[]{:S(2)}, u32[]{:S(2)}) collective-permute-start(bf16[16,128,128]{2,1,0:T(8,128)(2,1)S(1)} %all-to-all-done.refs_0_), channel_id=1, source_target_pairs={{0,48},{16,0},{32,16},{48,32},{64,112},{80,64},{96,80},{112,96},{1... | collective-permute-start | bytes 1572872 | tf_op jit(solution)/shard_map/gather_blocks/ppermute | solution.py:174
  57.9 1.6 %copy-done = bf16[64,128,128]{2,1,0:T(8,128)(2,1)S(1)} copy-done((bf16[64,128,128]{2,1,0:T(8,128)(2,1)S(1)}, bf16[64,128,128]{2,1,0:T(8,128)(2,1)}, u32[]{:S(2)}) %copy-start) | copy-done | bytes 2097176
  60.5 3.4 %terms.1 = (bf16[16,128,128]{2,1,0:T(8,128)(2,1)S(1)}, bf16[16,128,128]{2,1,0:T(8,128)(2,1)S(1)}, bf16[16,128,128]{2,1,0:T(8,128)(2,1)S(1)}, bf16[16,128,128]{2,1,0:T(8,128)(2,1)S(1)}, bf16[32,128,128]{2,1,0:T(8,128)(2,1)S(1)}) custom-call(s32[96]{0:T(128)S(1)} %bitcast.15, s32[96]{0:T(128)S(1)} %bitcast.18, s32[2]{0:T(128)S(1)} %pad_add_fusion.me_ref, ...), custom_call_target="tpu_custom_call" | custom-call | flops 1610612736 | bytes 6000000 | tf_op jit(solution)/shard_map/terms/pallas_call | solution.py:34
  65.8 7.0 %collective-permute-done.1.refs_2_ = bf16[16,128,128]{2,1,0:T(8,128)(2,1)S(1)} collective-permute-done((bf16[16,128,128]{2,1,0:T(8,128)(2,1)S(1)}, bf16[16,128,128]{2,1,0:T(8,128)(2,1)S(1)}, u32[]{:S(2)}, u32[]{:S(2)}) %collective-permute-start.1) | collective-permute-done | bytes 524320 | tf_op jit(solution)/shard_map/gather_blocks/ppermute | solution.py:174
  72.8 1.6 %collective-permute-done.2.refs_3_ = bf16[16,128,128]{2,1,0:T(8,128)(2,1)} collective-permute-done((bf16[16,128,128]{2,1,0:T(8,128)(2,1)S(1)}, bf16[16,128,128]{2,1,0:T(8,128)(2,1)}, u32[]{:S(2)}, u32[]{:S(2)}) %collective-permute-start.2) | collective-permute-done | bytes 524320 | tf_op jit(solution)/shard_map/gather_blocks/ppermute | solution.py:174
  75.4 5.7 %forward.1 = bf16[64,128,128]{2,1,0:T(8,128)(2,1)} custom-call(s32[96]{0:T(128)S(1)} %bitcast.16, s32[96]{0:T(128)S(1)} %bitcast.19, s32[2]{0:T(128)S(1)} %pad_add_fusion.me_ref, bf16[13,128,128]{2,1,0:T(8,128)(2,1)S(1)} %copy-done.17, bf16[16,128,128]{2,1,0:T(8,128)(2,1)S(1)} %all-to-all-done.refs_0_, ...), custom_call_target="tpu_custom_call" | custom-call | flops 1610612736 | bytes 6000000 | tf_op jit(solution)/shard_map/forward/pallas_call | solution.py:34
  81.1 6.8 %all-to-all-start.3 = ((bf16[32,128,128]{2,1,0:T(8,128)(2,1)}), bf16[32,128,128]{2,1,0:T(8,128)(2,1)S(1)}, u32[]{:S(2)}, u32[]{:S(2)}) async-start(bf16[32,128,128]{2,1,0:T(8,128)(2,1)} %copy-done.2), calls=%async_computation.4 | async-start | bytes 2097152 | tf_op jit(solution)/shard_map/sum_terms_first/all_to_all | solution.py:152
  88.0 4.3 %collective-permute-start.6 = (bf16[16,128,128]{2,1,0:T(8,128)(2,1)}, bf16[16,128,128]{2,1,0:T(8,128)(2,1)S(1)}, u32[]{:S(2)}, u32[]{:S(2)}) collective-permute-start(bf16[16,128,128]{2,1,0:T(8,128)(2,1)} %copy-done.15), channel_id=1, source_target_pairs={{0,16},{16,32},{32,48},{48,0},{64,80},{80,96},{96,112},{112,64},{1... | collective-permute-start | bytes 1572872 | tf_op jit(solution)/shard_map/sum_terms_first/ppermute | solution.py:182
  92.2 3.6 %collective-permute-start.7 = (bf16[16,128,128]{2,1,0:T(8,128)(2,1)}, bf16[16,128,128]{2,1,0:T(8,128)(2,1)S(1)}, u32[]{:S(2)}, u32[]{:S(2)}) collective-permute-start(bf16[16,128,128]{2,1,0:T(8,128)(2,1)} %copy-done.14), channel_id=1, source_target_pairs={{0,32},{16,48},{32,0},{48,16},{64,96},{80,112},{96,64},{112,80},{1... | collective-permute-start | bytes 1572872 | tf_op jit(solution)/shard_map/sum_terms_first/ppermute | solution.py:182
  95.9 3.5 %collective-permute-start.8 = (bf16[16,128,128]{2,1,0:T(8,128)(2,1)}, bf16[16,128,128]{2,1,0:T(8,128)(2,1)S(1)}, u32[]{:S(2)}, u32[]{:S(2)}) collective-permute-start(bf16[16,128,128]{2,1,0:T(8,128)(2,1)} %copy-done.13), channel_id=1, source_target_pairs={{0,48},{16,0},{32,16},{48,32},{64,112},{80,64},{96,80},{112,96},{1... | collective-permute-start | bytes 1572872 | tf_op jit(solution)/shard_map/sum_terms_first/ppermute | solution.py:182
  99.3 5.5 %collective-permute-done.6 = bf16[16,128,128]{2,1,0:T(8,128)(2,1)S(1)} collective-permute-done((bf16[16,128,128]{2,1,0:T(8,128)(2,1)}, bf16[16,128,128]{2,1,0:T(8,128)(2,1)S(1)}, u32[]{:S(2)}, u32[]{:S(2)}) %collective-permute-start.6) | collective-permute-done | bytes 524320 | tf_op jit(solution)/shard_map/sum_terms_first/ppermute | solution.py:182
  104.9 12.0 %collective-permute-done.7 = bf16[16,128,128]{2,1,0:T(8,128)(2,1)S(1)} collective-permute-done((bf16[16,128,128]{2,1,0:T(8,128)(2,1)}, bf16[16,128,128]{2,1,0:T(8,128)(2,1)S(1)}, u32[]{:S(2)}, u32[]{:S(2)}) %collective-permute-start.7) | collective-permute-done | bytes 524320 | tf_op jit(solution)/shard_map/sum_terms_first/ppermute | solution.py:182
  116.9 1.4 collective-permute-done.8
  118.3 1.1 add_convert_fusion
  119.4 6.9 %all-to-all-start.2 = ((bf16[16,128,128]{2,1,0:T(8,128)(2,1)}), bf16[16,128,128]{2,1,0:T(8,128)(2,1)S(1)}, u32[]{:S(2)}, u32[]{:S(2)}) async-start(bf16[16,128,128]{2,1,0:T(8,128)(2,1)} %add_convert_fusion), calls=%async_computation.3 | async-start | bytes 1048576 | tf_op jit(solution)/shard_map/sum_terms_second/all_to_all | solution.py:152
  126.5 4.9 %collective-permute-start.10 = (bf16[1,128,128]{2,1,0:T(8,128)(2,1)S(1)}, bf16[1,128,128]{2,1,0:T(8,128)(2,1)S(1)}, u32[]{:S(2)}, u32[]{:S(2)}) collective-permute-start(bf16[1,128,128]{2,1,0:T(8,128)(2,1)S(1)} %get-tuple-element.44), channel_id=1, source_target_pairs={{0,32},{16,48},{32,0},{48,16},{64,96},{80,112},{96,64},{112,80},{1... | collective-permute-start | bytes 98312 | tf_op jit(solution)/shard_map/sum_terms_second/ppermute | solution.py:202
  131.4 3.9 %collective-permute-start.11 = (bf16[1,128,128]{2,1,0:T(8,128)(2,1)S(1)}, bf16[1,128,128]{2,1,0:T(8,128)(2,1)S(1)}, u32[]{:S(2)}, u32[]{:S(2)}) collective-permute-start(bf16[1,128,128]{2,1,0:T(8,128)(2,1)S(1)} %get-tuple-element.45), channel_id=1, source_target_pairs={{0,48},{16,0},{32,16},{48,32},{64,112},{80,64},{96,80},{112,96},{1... | collective-permute-start | bytes 98312 | tf_op jit(solution)/shard_map/sum_terms_second/ppermute | solution.py:202
  135.4 1.9 %collective-permute-start.9 = (bf16[1,128,128]{2,1,0:T(8,128)(2,1)S(1)}, bf16[1,128,128]{2,1,0:T(8,128)(2,1)S(1)}, u32[]{:S(2)}, u32[]{:S(2)}) collective-permute-start(bf16[1,128,128]{2,1,0:T(8,128)(2,1)S(1)} %get-tuple-element.43), channel_id=1, source_target_pairs={{0,16},{16,32},{32,48},{48,0},{64,80},{80,96},{96,112},{112,64},{1... | collective-permute-start | bytes 98312 | tf_op jit(solution)/shard_map/sum_terms_second/ppermute | solution.py:202
  137.3 1.6 %copy-done.1 = bf16[64,128,128]{2,1,0:T(8,128)(2,1)S(1)} copy-done((bf16[64,128,128]{2,1,0:T(8,128)(2,1)S(1)}, bf16[64,128,128]{2,1,0:T(8,128)(2,1)}, u32[]{:S(2)}) %copy-start.1) | copy-done | bytes 2097176
  138.9 1.0 copy-done.4
  139.9 1.0 copy-done.6
  143.0 6.1 %backward.1 = (bf16[128,1664]{1,0:T(8,128)(2,1)}, bf16[128,1664]{1,0:T(8,128)(2,1)}) custom-call(s32[96]{0:T(128)S(1)} %bitcast.17, s32[96]{0:T(128)S(1)} %bitcast.20, s32[2]{0:T(128)S(1)} %pad_add_fusion.me_ref, bf16[64,128,128]{2,1,0:T(8,128)(2,1)S(1)} %copy-done.1, bf16[128,1664]{1,0:T(8,128)(2,1)S(1)} %copy-done.8, bf16[128,1664]{1,0:T(8,128)(2,1)S(1)} %copy-done.10, ...), custom_call_target="tpu_custom_call" | custom-call | flops 1610612736 | bytes 8000000 | tf_op jit(solution)/shard_map/backward/pallas_call | solution.py:34
  (63 shorter events, 15.9 us)
Async XLA Ops:
  7.2 50.7 %all-gather.2.cloned.1.call-start = ((), (), s32[]{:S(2)}) async-start(), calls=%async_computation.5 | async-start | bytes 2228224 | tf_op jit(solution)/shard_map/gather_out_grad/all_gather | solution.py:168
  10.8 44.2 %copy-start.7 = (bf16[128,1664]{1,0:T(8,128)(2,1)S(1)}, bf16[128,1664]{1,0:T(8,128)(2,1)}, u32[]{:S(2)}) copy-start(bf16[128,1664]{1,0:T(8,128)(2,1)} %gate_ref.3) | copy-start | bytes 1277956
  10.8 27.9 %all-to-all-start = ((bf16[16,128,128]{2,1,0:T(8,128)(2,1)}), bf16[16,128,128]{2,1,0:T(8,128)(2,1)S(1)}, u32[]{:S(2)}, u32[]{:S(2)}) async-start(bf16[16,128,128]{2,1,0:T(8,128)(2,1)} %bitcast.7), calls=%async_computation | async-start | bytes 1048576 | tf_op jit(solution)/shard_map/gather_blocks/all_to_all | solution.py:152
  22.0 11.4 %collective-permute-start.3 = (bf16[1,128,128]{2,1,0:T(8,128)(2,1)S(1)}, bf16[1,128,128]{2,1,0:T(8,128)(2,1)S(1)}, u32[]{:S(2)}, u32[]{:S(2)}) collective-permute-start(bf16[1,128,128]{2,1,0:T(8,128)(2,1)S(1)} %slice.7), channel_id=1, source_target_pairs={{0,16},{16,32},{32,48},{48,0},{64,80},{80,96},{96,112},{112,64},{1... | collective-permute-start | bytes 98312 | tf_op jit(solution)/shard_map/gather_blocks/ppermute | solution.py:172
  25.4 8.0 %collective-permute-start.4 = (bf16[1,128,128]{2,1,0:T(8,128)(2,1)S(1)}, bf16[1,128,128]{2,1,0:T(8,128)(2,1)S(1)}, u32[]{:S(2)}, u32[]{:S(2)}) collective-permute-start(bf16[1,128,128]{2,1,0:T(8,128)(2,1)S(1)} %slice.7), channel_id=1, source_target_pairs={{0,32},{16,48},{32,0},{48,16},{64,96},{80,112},{96,64},{112,80},{1... | collective-permute-start | bytes 98312 | tf_op jit(solution)/shard_map/gather_blocks/ppermute | solution.py:172
  30.1 5.8 %collective-permute-start.5 = (bf16[1,128,128]{2,1,0:T(8,128)(2,1)S(1)}, bf16[1,128,128]{2,1,0:T(8,128)(2,1)S(1)}, u32[]{:S(2)}, u32[]{:S(2)}) collective-permute-start(bf16[1,128,128]{2,1,0:T(8,128)(2,1)S(1)} %slice.7), channel_id=1, source_target_pairs={{0,48},{16,0},{32,16},{48,32},{64,112},{80,64},{96,80},{112,96},{1... | collective-permute-start | bytes 98312 | tf_op jit(solution)/shard_map/gather_blocks/ppermute | solution.py:172
  39.9 34.5 %all-to-all-start.1 = ((bf16[32,128,128]{2,1,0:T(8,128)(2,1)}), bf16[32,128,128]{2,1,0:T(8,128)(2,1)S(1)}, u32[]{:S(2)}, u32[]{:S(2)}) async-start(bf16[32,128,128]{2,1,0:T(8,128)(2,1)} %bitcast.8), calls=%async_computation.1 | async-start | bytes 2097152 | tf_op jit(solution)/shard_map/gather_blocks/all_to_all | solution.py:152
  44.3 13.6 %copy-start.11 = (s32[96,1]{0,1:T(1,128)S(1)}, s32[96,1]{0,1:T(1,128)}, u32[]{:S(2)}) copy-start(s32[96,1]{0,1:T(1,128)} %param.10) | copy-start | bytes 1156
  44.3 13.6 %copy-start.12 = (s32[96,1]{0,1:T(1,128)S(1)}, s32[96,1]{0,1:T(1,128)}, u32[]{:S(2)}) copy-start(s32[96,1]{0,1:T(1,128)} %param.11) | copy-start | bytes 1156
  44.3 105.6 %reduce-scatter.2.cloned.1.call-start = ((), (), s32[]{:S(2)}) async-start(), calls=%async_computation.6 | async-start | bytes 2228224 | tf_op jit(solution)/shard_map/sum_output/reduce_scatter | solution.py:190
  44.4 21.4 %collective-permute-start = (bf16[16,128,128]{2,1,0:T(8,128)(2,1)S(1)}, bf16[16,128,128]{2,1,0:T(8,128)(2,1)S(1)}, u32[]{:S(2)}, u32[]{:S(2)}) collective-permute-start(bf16[16,128,128]{2,1,0:T(8,128)(2,1)S(1)} %all-to-all-done.refs_0_), channel_id=1, source_target_pairs={{0,16},{16,32},{32,48},{48,0},{64,80},{80,96},{96,112},{112,64},{1... | collective-permute-start | bytes 1572872 | tf_op jit(solution)/shard_map/gather_blocks/ppermute | solution.py:174
  47.0 25.8 %collective-permute-start.1 = (bf16[16,128,128]{2,1,0:T(8,128)(2,1)S(1)}, bf16[16,128,128]{2,1,0:T(8,128)(2,1)S(1)}, u32[]{:S(2)}, u32[]{:S(2)}) collective-permute-start(bf16[16,128,128]{2,1,0:T(8,128)(2,1)S(1)} %all-to-all-done.refs_0_), channel_id=1, source_target_pairs={{0,32},{16,48},{32,0},{48,16},{64,96},{80,112},{96,64},{112,80},{1... | collective-permute-start | bytes 1572872 | tf_op jit(solution)/shard_map/gather_blocks/ppermute | solution.py:174
  52.3 22.1 %collective-permute-start.2 = (bf16[16,128,128]{2,1,0:T(8,128)(2,1)S(1)}, bf16[16,128,128]{2,1,0:T(8,128)(2,1)}, u32[]{:S(2)}, u32[]{:S(2)}) collective-permute-start(bf16[16,128,128]{2,1,0:T(8,128)(2,1)S(1)} %all-to-all-done.refs_0_), channel_id=1, source_target_pairs={{0,48},{16,0},{32,16},{48,32},{64,112},{80,64},{96,80},{112,96},{1... | collective-permute-start | bytes 1572872 | tf_op jit(solution)/shard_map/gather_blocks/ppermute | solution.py:174
  55.0 1.0 copy-start.9
  57.9 1.6 %copy-start = (bf16[64,128,128]{2,1,0:T(8,128)(2,1)S(1)}, bf16[64,128,128]{2,1,0:T(8,128)(2,1)}, u32[]{:S(2)}) copy-start(bf16[64,128,128]{2,1,0:T(8,128)(2,1)} %all-gather.2.cloned.1.call-done.grad_ref) | copy-start | bytes 6291460
  59.5 1.0 copy-start.19
  65.8 7.0 %copy-start.13 = (bf16[16,128,128]{2,1,0:T(8,128)(2,1)}, bf16[16,128,128]{2,1,0:T(8,128)(2,1)S(1)}, u32[]{:S(2)}) copy-start(bf16[16,128,128]{2,1,0:T(8,128)(2,1)S(1)} %get-tuple-element.40) | copy-start | bytes 1572868
  65.8 7.0 %copy-start.14 = (bf16[16,128,128]{2,1,0:T(8,128)(2,1)}, bf16[16,128,128]{2,1,0:T(8,128)(2,1)S(1)}, u32[]{:S(2)}) copy-start(bf16[16,128,128]{2,1,0:T(8,128)(2,1)S(1)} %get-tuple-element.39) | copy-start | bytes 1572868
  65.8 15.3 %copy-start.3 = (bf16[16,128,128]{2,1,0:T(8,128)(2,1)}, bf16[16,128,128]{2,1,0:T(8,128)(2,1)S(1)}, u32[]{:S(2)}) copy-start(bf16[16,128,128]{2,1,0:T(8,128)(2,1)S(1)} %collective-permute-done.refs_1_) | copy-start | bytes 1572868
  72.8 8.3 %copy-start.5 = (bf16[16,128,128]{2,1,0:T(8,128)(2,1)}, bf16[16,128,128]{2,1,0:T(8,128)(2,1)S(1)}, u32[]{:S(2)}) copy-start(bf16[16,128,128]{2,1,0:T(8,128)(2,1)S(1)} %collective-permute-done.1.refs_2_) | copy-start | bytes 1572868
  74.4 1.0 copy-start.17
  81.1 38.3 %all-to-all-start.3 = ((bf16[32,128,128]{2,1,0:T(8,128)(2,1)}), bf16[32,128,128]{2,1,0:T(8,128)(2,1)S(1)}, u32[]{:S(2)}, u32[]{:S(2)}) async-start(bf16[32,128,128]{2,1,0:T(8,128)(2,1)} %copy-done.2), calls=%async_computation.4 | async-start | bytes 2097152 | tf_op jit(solution)/shard_map/sum_terms_first/all_to_all | solution.py:152
  88.0 16.9 %collective-permute-start.6 = (bf16[16,128,128]{2,1,0:T(8,128)(2,1)}, bf16[16,128,128]{2,1,0:T(8,128)(2,1)S(1)}, u32[]{:S(2)}, u32[]{:S(2)}) collective-permute-start(bf16[16,128,128]{2,1,0:T(8,128)(2,1)} %copy-done.15), channel_id=1, source_target_pairs={{0,16},{16,32},{32,48},{48,0},{64,80},{80,96},{96,112},{112,64},{1... | collective-permute-start | bytes 1572872 | tf_op jit(solution)/shard_map/sum_terms_first/ppermute | solution.py:182
  92.2 24.7 %collective-permute-start.7 = (bf16[16,128,128]{2,1,0:T(8,128)(2,1)}, bf16[16,128,128]{2,1,0:T(8,128)(2,1)S(1)}, u32[]{:S(2)}, u32[]{:S(2)}) collective-permute-start(bf16[16,128,128]{2,1,0:T(8,128)(2,1)} %copy-done.14), channel_id=1, source_target_pairs={{0,32},{16,48},{32,0},{48,16},{64,96},{80,112},{96,64},{112,80},{1... | collective-permute-start | bytes 1572872 | tf_op jit(solution)/shard_map/sum_terms_first/ppermute | solution.py:182
  95.9 22.4 %collective-permute-start.8 = (bf16[16,128,128]{2,1,0:T(8,128)(2,1)}, bf16[16,128,128]{2,1,0:T(8,128)(2,1)S(1)}, u32[]{:S(2)}, u32[]{:S(2)}) collective-permute-start(bf16[16,128,128]{2,1,0:T(8,128)(2,1)} %copy-done.13), channel_id=1, source_target_pairs={{0,48},{16,0},{32,16},{48,32},{64,112},{80,64},{96,80},{112,96},{1... | collective-permute-start | bytes 1572872 | tf_op jit(solution)/shard_map/sum_terms_first/ppermute | solution.py:182
  119.4 29.7 %all-to-all-start.2 = ((bf16[16,128,128]{2,1,0:T(8,128)(2,1)}), bf16[16,128,128]{2,1,0:T(8,128)(2,1)S(1)}, u32[]{:S(2)}, u32[]{:S(2)}) async-start(bf16[16,128,128]{2,1,0:T(8,128)(2,1)} %add_convert_fusion), calls=%async_computation.3 | async-start | bytes 1048576 | tf_op jit(solution)/shard_map/sum_terms_second/all_to_all | solution.py:152
  126.5 22.7 %collective-permute-start.10 = (bf16[1,128,128]{2,1,0:T(8,128)(2,1)S(1)}, bf16[1,128,128]{2,1,0:T(8,128)(2,1)S(1)}, u32[]{:S(2)}, u32[]{:S(2)}) collective-permute-start(bf16[1,128,128]{2,1,0:T(8,128)(2,1)S(1)} %get-tuple-element.44), channel_id=1, source_target_pairs={{0,32},{16,48},{32,0},{48,16},{64,96},{80,112},{96,64},{112,80},{1... | collective-permute-start | bytes 98312 | tf_op jit(solution)/shard_map/sum_terms_second/ppermute | solution.py:202
  131.4 17.7 %collective-permute-start.11 = (bf16[1,128,128]{2,1,0:T(8,128)(2,1)S(1)}, bf16[1,128,128]{2,1,0:T(8,128)(2,1)S(1)}, u32[]{:S(2)}, u32[]{:S(2)}) collective-permute-start(bf16[1,128,128]{2,1,0:T(8,128)(2,1)S(1)} %get-tuple-element.45), channel_id=1, source_target_pairs={{0,48},{16,0},{32,16},{48,32},{64,112},{80,64},{96,80},{112,96},{1... | collective-permute-start | bytes 98312 | tf_op jit(solution)/shard_map/sum_terms_second/ppermute | solution.py:202
  135.4 13.8 %collective-permute-start.9 = (bf16[1,128,128]{2,1,0:T(8,128)(2,1)S(1)}, bf16[1,128,128]{2,1,0:T(8,128)(2,1)S(1)}, u32[]{:S(2)}, u32[]{:S(2)}) collective-permute-start(bf16[1,128,128]{2,1,0:T(8,128)(2,1)S(1)} %get-tuple-element.43), channel_id=1, source_target_pairs={{0,16},{16,32},{32,48},{48,0},{64,80},{80,96},{96,112},{112,64},{1... | collective-permute-start | bytes 98312 | tf_op jit(solution)/shard_map/sum_terms_second/ppermute | solution.py:202
  137.3 1.6 %copy-start.1 = (bf16[64,128,128]{2,1,0:T(8,128)(2,1)S(1)}, bf16[64,128,128]{2,1,0:T(8,128)(2,1)}, u32[]{:S(2)}) copy-start(bf16[64,128,128]{2,1,0:T(8,128)(2,1)} %all-gather.2.cloned.1.call-done.grad_ref) | copy-start | bytes 6291460
  138.9 1.0 copy-start.4
  139.9 1.1 copy-start.6
  (6 other events, 5.4 us)
Sparse Core Ops, SparseCore 0:
  10.7 44.6 all-gather.1
  81.2 59.5 reduce-scatter.1

commit v2 on v1

--- a/solution.py
+++ b/solution.py
@@ -27,6 +27,7 @@
 
 CORE_SWAP = [(t, t ^ 1) for t in range(2 * NY)]
 Z_GROUPS = [[z * NX + x for z in range(NZ)] for x in range(NX)]
+X_GROUPS = [[z * NX + x for x in range(NX)] for z in range(NZ)]
 Y_GROUPS = [[y * 2 + c for y in range(NY)] for c in range(2)]
 
 
@@ -76,17 +77,22 @@
         hid_t_ref[r] = hidden.T.astype(jnp.bfloat16)
 
 
-def terms_kernel(rows_ref, cols_ref, me_ref, hid_t_ref, grad_ref, *out_refs):
-    def visit(ref, entries):
-        for i, k in entries:
-            ref[i] = jnp.dot(
+def terms_kernel(rows_ref, cols_ref, hid_t_ref, grad_ref, out_ref):
+    def some(g, carry):
+        for j in range(STEP):
+            i = g * STEP + j
+            z, place = lax.rem(i // OWNED, NZ), lax.rem(i, OWNED)
+            k = block_of(z, i // (NZ * OWNED), place)
+            out_ref[i] = jnp.dot(
                 hid_t_ref[rows_ref[k]], grad_ref[cols_ref[k]], preferred_element_type=jnp.float32
             ).astype(jnp.bfloat16)
-    each_block(out_refs, me_ref[0], 1, visit)
+        return carry
+    lax.fori_loop(0, GROUP_BLOCKS // STEP, some, 0)
 
 
 def forward_kernel(rows_ref, cols_ref, me_ref, hid_ref, *refs):
-    parts, (out_ref, total) = refs[:NX + 1], refs[NX + 1:]
+    parts, (keep_ref, send_ref, total) = refs[:NX + 1], refs[NX + 1:]
+    core = me_ref[1]
     total[...] = jnp.zeros_like(total)
 
     def visit(ref, entries):
@@ -98,8 +104,10 @@
     each_block(parts, me_ref[0], -1, visit)
 
     def put(y, carry):
-        for j in range(8):
-            out_ref[y * 8 + j] = total[y * 8 + j].astype(jnp.bfloat16)
+        mine, other = (y * 2 + core) * 4, (y * 2 + 1 - core) * 4
+        for j in range(4):
+            keep_ref[y * 4 + j] = total[mine + j].astype(jnp.bfloat16)
+            send_ref[y * 4 + j] = total[other + j].astype(jnp.bfloat16)
         return carry
     lax.fori_loop(0, NY, put, 0)
 
@@ -127,29 +135,20 @@
         d_up_ref[:, here] = (back * gate * sigma).astype(jnp.bfloat16)
 
 
-def near_sum_kernel(arrived_ref, *out_refs):
-    for b, out_ref in enumerate(out_refs):
-        total = arrived_ref[b].astype(jnp.float32)
-        for z in range(1, NZ):
-            total += arrived_ref[z * NX + b].astype(jnp.float32)
-        out_ref[0] = total.astype(jnp.bfloat16)
-
-
-def block_sum_kernel(far_ref, *refs):
-    near_refs, out_ref = refs[:NX], refs[NX]
-    for j in range(FAR):
-        total = far_ref[j].astype(jnp.float32)
-        for z in range(1, NZ):
-            total += far_ref[z * FAR + j].astype(jnp.float32)
-        out_ref[j] = total
-    total = near_refs[0][0].astype(jnp.float32)
-    for ref in near_refs[1:]:
-        total += ref[0].astype(jnp.float32)
-    out_ref[FAR] = total
-
-
-def z_exchange(a):
-    return lax.all_to_all(a, "fsdp", 0, 0, tiled=True, axis_index_groups=Z_GROUPS)
+def sum_kernel(parts, arrived_ref, out_ref):
+    n = out_ref.shape[0]
+
+    def some(j, carry):
+        total = arrived_ref[j].astype(jnp.float32)
+        for p in range(1, parts):
+            total += arrived_ref[p * n + j].astype(jnp.float32)
+        out_ref[j] = total.astype(out_ref.dtype)
+        return carry
+    lax.fori_loop(0, n, some, 0)
+
+
+def exchange(a, groups):
+    return lax.all_to_all(a, "fsdp", 0, 0, tiled=True, axis_index_groups=groups)
 
 
 def to_all(a):
@@ -167,40 +166,40 @@
         grad_tiles, blocks = lax.optimization_barrier((grad_tiles, blocks))
         grad_tiles = lax.all_gather(grad_tiles, "tensor", axis=0, tiled=True)
     with jax.named_scope("gather_blocks"):
-        far = z_exchange(to_all(blocks[:FAR]))
+        far = exchange(to_all(blocks[:FAR]), Z_GROUPS)
         near = blocks[FAR:]
         near = jnp.concatenate([near] + [lax.ppermute(near, "fsdp", x_shift(s)) for s in range(1, NX)], axis=0)
-        near = z_exchange(to_all(near))
+        near = exchange(to_all(near), Z_GROUPS)
         parts = [far] + [lax.ppermute(far, "fsdp", x_shift(s)) for s in range(1, NX)] + [near]
     with jax.named_scope("hidden"):
         hid, hid_t = call(hidden_kernel, (tiles(HID_TILES), tiles(HID_TILES)), (gate_pre, up_pre), flops=10**9, moved=4 * 10**6)
     with jax.named_scope("terms"):
-        outs = tuple(tiles(NZ * FAR) for _ in range(NX)) + (tiles(NZ * NX),)
-        terms = call(terms_kernel, outs, (rows, cols, me, hid_t, grad_tiles), flops=8 * macs, moved=6 * 10**6)
+        terms = call(terms_kernel, tiles(GROUP_BLOCKS), (rows, cols, hid_t, grad_tiles), flops=8 * macs, moved=6 * 10**6)
         terms, hid = lax.optimization_barrier((terms, hid))
-    with jax.named_scope("sum_terms_first"):
-        far_terms = [terms[0]] + [lax.ppermute(terms[s], "fsdp", x_shift(s)) for s in range(1, NX)]
-        near_terms = z_exchange(terms[NX])
+    with jax.named_scope("sum_terms_x"):
+        terms = exchange(terms, X_GROUPS)
     with jax.named_scope("forward"):
-        summed = call(
-            forward_kernel, tiles(64), (rows, cols, me, hid, *parts),
+        keep, send = call(
+            forward_kernel, (tiles(32), tiles(32)), (rows, cols, me, hid, *parts),
             scratch=[pltpu.VMEM((WIDTH_TILES, BLK, BLK), jnp.float32)], flops=8 * macs, moved=6 * 10**6,
         )
     with jax.named_scope("sum_output"):
-        output = lax.psum_scatter(summed, "tensor", scatter_dimension=0, tiled=True)
+        swapped = lax.ppermute(send, "tensor", CORE_SWAP)
+        pair = (keep.astype(jnp.float32) + swapped.astype(jnp.float32)).astype(jnp.bfloat16)
+        pair, me_late = lax.optimization_barrier((pair, me))
+        output = lax.psum_scatter(pair, "tensor", scatter_dimension=0, axis_index_groups=Y_GROUPS, tiled=True)
         output = output.transpose(1, 0, 2).reshape(BLK, 4 * BLK)
     with jax.named_scope("backward"):
         wide = jax.ShapeDtypeStruct(gate_pre.shape, jnp.bfloat16)
         d_gate, d_up = call(
-            backward_kernel, (wide, wide), (rows, cols, me, grad_tiles, gate_pre, up_pre, *parts),
+            backward_kernel, (wide, wide), (rows, cols, me_late, grad_tiles, gate_pre, up_pre, *parts),
             scratch=[pltpu.VMEM((HID_TILES, BLK, BLK), jnp.float32)], flops=8 * macs, moved=8 * 10**6,
         )
-    with jax.named_scope("sum_terms_second"):
-        far_terms = functools.reduce(jnp.add, [a.astype(jnp.float32) for a in far_terms]).astype(jnp.bfloat16)
-        far_terms = z_exchange(far_terms)
-        near_terms = call(near_sum_kernel, tuple(tiles(1) for _ in range(NX)), (near_terms,), moved=10**6)
-        near_terms = [near_terms[0]] + [lax.ppermute(near_terms[s], "fsdp", x_shift(s)) for s in range(1, NX)]
-        grad_blocks = call(block_sum_kernel, tiles(OWNED, jnp.float32), (far_terms, *near_terms), moved=10**6)
+    with jax.named_scope("sum_terms_z"):
+        terms, d_gate, d_up = lax.optimization_barrier((terms, d_gate, d_up))
+        terms = call(functools.partial(sum_kernel, NX), tiles(NZ * OWNED), (terms,), moved=4 * 10**6)
+        terms = exchange(terms, Z_GROUPS)
+        grad_blocks = call(functools.partial(sum_kernel, NZ), tiles(OWNED, jnp.float32), (terms,), moved=10**6)
         grad_blocks = grad_blocks.reshape(OWNED, 1, BLK, BLK)
     return (output, d_gate, d_up, grad_blocks)
 

time: 160 us -> 153 us (0.956)
  starting transfers between devices: 72.7 us -> 46.6 us
  waiting for transfers between devices: 32.9 us -> 52.1 us
    all_to_all x4, waiting for transfers between devices: 2.87 us -> 38 us  [exchange(): return lax.all_to_all(a, 'fsdp', 0, 0, tiled=True, axis_index_groups=groups)]
    ppermute x6 -> x1, starting transfers between devices: 22.1 us -> 1.92 us  [shards(): swapped = lax.ppermute(send, 'tensor', CORE_SWAP)]
    ppermute x6 -> x1, waiting for transfers between devices: 18.9 us -> 2.63 us  [shards(): swapped = lax.ppermute(send, 'tensor', CORE_SWAP)]
    reduce_scatter x1, waiting for transfers between devices: 0.01 us -> 8.96 us  [shards(): lax.psum_scatter(pair, 'tensor', scatter_dimension=0, axis_index_groups=Y...]
    ppermute x3, waiting for transfers between devices: 8.63 us -> 0.01 us  [shards(): lax.ppermute(far, 'fsdp', x_shift(s))]
    all_to_all x4, starting transfers between devices: 28.6 us -> 22.6 us  [exchange(): return lax.all_to_all(a, 'fsdp', 0, 0, tiled=True, axis_index_groups=groups)]
    unnamed x42 -> x32, local copies, waits for them, and re-layouts: 15.5 us -> 14 us
  transfers between devices with their start and end apart: 18 -> 13, of which waited for: 7 -> 8; matrix products, arithmetic and copies ran while one was open for 3% -> 5% of each run, Pallas kernels for 7% -> 11%
where the time goes in v2:
time: 153 us; the launch traced here: 151 us
  waiting for transfers between devices  52.1 us (34%)
  starting transfers between devices  46.6 us (30%)
  local copies, waits for them, and re-layouts  19.5 us (13%)
  Pallas kernels  16.6 us (11%)
  between operations  14.2 us (9%)
  other arithmetic  1.56 us (1%)
    all_to_all x4, waiting for transfers between devices, exchange(): return lax.all_to_all(a, 'fsdp', 0, 0, tiled=True, axis_index_groups=groups)  38 us
    all_to_all x4, starting transfers between devices, exchange(): return lax.all_to_all(a, 'fsdp', 0, 0, tiled=True, axis_index_groups=groups)  22.6 us
    pallas_call x6, Pallas kernels, call(): pl.pallas_call(kernel, out_shape=outs, in_specs=[SMEM if a.dtype == jnp.i...  16.6 us
    unnamed x32, local copies, waits for them, and re-layouts  14 us
    ppermute x3, starting transfers between devices, shards(): lax.ppermute(near, 'fsdp', x_shift(s))  11.4 us
    ppermute x3, starting transfers between devices, shards(): lax.ppermute(far, 'fsdp', x_shift(s))  10.7 us
    reduce_scatter x1, waiting for transfers between devices, shards(): lax.psum_scatter(pair, 'tensor', scatter_dimension=0, axis_index_groups=Y...  8.96 us
  transfers between devices with their start and end apart: 13, of which 8 were waited for; matrix products, arithmetic and copies ran while one was open for 5% of the time, Pallas kernels for 11%

profile of v2, /device:TPU:56, one launch (start us, length us, event | category | flops | bytes accessed | tf_op | source)
XLA Modules:
  0.0 150.7 jit_solution(14670135160572841314)
XLA Ops:
  7.2 1.0 copy.16
  10.8 10.4 %all-to-all-start = ((bf16[16,128,128]{2,1,0:T(8,128)(2,1)}), bf16[16,128,128]{2,1,0:T(8,128)(2,1)}, u32[]{:S(2)}, u32[]{:S(2)}) async-start(bf16[16,128,128]{2,1,0:T(8,128)(2,1)} %bitcast.7), calls=%async_computation | async-start | bytes 1048576 | tf_op jit(solution)/shard_map/gather_blocks/all_to_all | solution.py:151
  22.0 3.4 %collective-permute-start.3 = (bf16[1,128,128]{2,1,0:T(8,128)(2,1)S(1)}, bf16[1,128,128]{2,1,0:T(8,128)(2,1)S(1)}, u32[]{:S(2)}, u32[]{:S(2)}) collective-permute-start(bf16[1,128,128]{2,1,0:T(8,128)(2,1)S(1)} %slice.7), channel_id=1, source_target_pairs={{0,16},{16,32},{32,48},{48,0},{64,80},{80,96},{96,112},{112,64},{1... | collective-permute-start | bytes 98312 | tf_op jit(solution)/shard_map/gather_blocks/ppermute | solution.py:171
  25.4 4.6 %collective-permute-start.4 = (bf16[1,128,128]{2,1,0:T(8,128)(2,1)S(1)}, bf16[1,128,128]{2,1,0:T(8,128)(2,1)S(1)}, u32[]{:S(2)}, u32[]{:S(2)}) collective-permute-start(bf16[1,128,128]{2,1,0:T(8,128)(2,1)S(1)} %slice.7), channel_id=1, source_target_pairs={{0,32},{16,48},{32,0},{48,16},{64,96},{80,112},{96,64},{112,80},{1... | collective-permute-start | bytes 98312 | tf_op jit(solution)/shard_map/gather_blocks/ppermute | solution.py:171
  30.0 3.3 %collective-permute-start.5 = (bf16[1,128,128]{2,1,0:T(8,128)(2,1)S(1)}, bf16[1,128,128]{2,1,0:T(8,128)(2,1)S(1)}, u32[]{:S(2)}, u32[]{:S(2)}) collective-permute-start(bf16[1,128,128]{2,1,0:T(8,128)(2,1)S(1)} %slice.7), channel_id=1, source_target_pairs={{0,48},{16,0},{32,16},{48,32},{64,112},{80,64},{96,80},{112,96},{1... | collective-permute-start | bytes 98312 | tf_op jit(solution)/shard_map/gather_blocks/ppermute | solution.py:171
  33.4 2.4 %collective-permute-done.5 = bf16[1,128,128]{2,1,0:T(8,128)(2,1)S(1)} collective-permute-done((bf16[1,128,128]{2,1,0:T(8,128)(2,1)S(1)}, bf16[1,128,128]{2,1,0:T(8,128)(2,1)S(1)}, u32[]{:S(2)}, u32[]{:S(2)}) %collective-permute-start.5) | collective-permute-done | bytes 32800 | tf_op jit(solution)/shard_map/gather_blocks/ppermute | solution.py:171
  35.9 3.0 %all-to-all-done.refs_0_ = bf16[16,128,128]{2,1,0:T(8,128)(2,1)} async-done(((bf16[16,128,128]{2,1,0:T(8,128)(2,1)}), bf16[16,128,128]{2,1,0:T(8,128)(2,1)}, u32[]{:S(2)}, u32[]{:S(2)}) %all-to-all-start) | async-done | bytes 524320 | tf_op jit(solution)/shard_map/gather_blocks/all_to_all | solution.py:151
  38.8 1.2 broadcast_in_dim.5
  40.1 4.3 %all-to-all-start.1 = ((bf16[32,128,128]{2,1,0:T(8,128)(2,1)}), bf16[32,128,128]{2,1,0:T(8,128)(2,1)S(1)}, u32[]{:S(2)}, u32[]{:S(2)}) async-start(bf16[32,128,128]{2,1,0:T(8,128)(2,1)} %bitcast.8), calls=%async_computation.1 | async-start | bytes 2097152 | tf_op jit(solution)/shard_map/gather_blocks/all_to_all | solution.py:151
  44.3 2.7 %collective-permute-start = (bf16[16,128,128]{2,1,0:T(8,128)(2,1)}, bf16[16,128,128]{2,1,0:T(8,128)(2,1)}, u32[]{:S(2)}, u32[]{:S(2)}) collective-permute-start(bf16[16,128,128]{2,1,0:T(8,128)(2,1)} %all-to-all-done.refs_0_), channel_id=1, source_target_pairs={{0,16},{16,32},{32,48},{48,0},{64,80},{80,96},{96,112},{112,64},{1... | collective-permute-start | bytes 1572872 | tf_op jit(solution)/shard_map/gather_blocks/ppermute | solution.py:173
  47.1 5.3 %collective-permute-start.1 = (bf16[16,128,128]{2,1,0:T(8,128)(2,1)}, bf16[16,128,128]{2,1,0:T(8,128)(2,1)}, u32[]{:S(2)}, u32[]{:S(2)}) collective-permute-start(bf16[16,128,128]{2,1,0:T(8,128)(2,1)} %all-to-all-done.refs_0_), channel_id=1, source_target_pairs={{0,32},{16,48},{32,0},{48,16},{64,96},{80,112},{96,64},{112,80},{1... | collective-permute-start | bytes 1572872 | tf_op jit(solution)/shard_map/gather_blocks/ppermute | solution.py:173
  52.4 2.6 %collective-permute-start.2 = (bf16[16,128,128]{2,1,0:T(8,128)(2,1)}, bf16[16,128,128]{2,1,0:T(8,128)(2,1)}, u32[]{:S(2)}, u32[]{:S(2)}) collective-permute-start(bf16[16,128,128]{2,1,0:T(8,128)(2,1)} %all-to-all-done.refs_0_), channel_id=1, source_target_pairs={{0,48},{16,0},{32,16},{48,32},{64,112},{80,64},{96,80},{112,96},{1... | collective-permute-start | bytes 1572872 | tf_op jit(solution)/shard_map/gather_blocks/ppermute | solution.py:173
  55.5 1.7 %copy-done.5 = bf16[64,128,128]{2,1,0:T(8,128)(2,1)S(1)} copy-done((bf16[64,128,128]{2,1,0:T(8,128)(2,1)S(1)}, bf16[64,128,128]{2,1,0:T(8,128)(2,1)}, u32[]{:S(2)}) %copy-start.5) | copy-done | bytes 2097176
  57.2 3.6 %terms.1 = bf16[96,128,128]{2,1,0:T(8,128)(2,1)S(1)} custom-call(s32[96]{0:T(128)S(1)} %bitcast.15, s32[96]{0:T(128)S(1)} %bitcast.18, bf16[13,128,128]{2,1,0:T(8,128)(2,1)S(1)} %get-tuple-element.19.hid_t_ref, bf16[64,128,128]{2,1,0:T(8,128)(2,1)S(1)} %copy-done.5), custom_call_target="tpu_custom_call" | custom-call | flops 1610612736 | bytes 6000000 | tf_op jit(solution)/shard_map/terms/pallas_call | solution.py:35
  60.8 1.6 %copy-done.3 = bf16[96,128,128]{2,1,0:T(8,128)(2,1)} copy-done((bf16[96,128,128]{2,1,0:T(8,128)(2,1)}, bf16[96,128,128]{2,1,0:T(8,128)(2,1)S(1)}, u32[]{:S(2)}) %copy-start.3) | copy-done | bytes 3145752
  62.4 10.3 %all-to-all-done.1.refs_4_ = bf16[32,128,128]{2,1,0:T(8,128)(2,1)S(1)} async-done(((bf16[32,128,128]{2,1,0:T(8,128)(2,1)}), bf16[32,128,128]{2,1,0:T(8,128)(2,1)S(1)}, u32[]{:S(2)}, u32[]{:S(2)}) %all-to-all-start.1) | async-done | bytes 1048608 | tf_op jit(solution)/shard_map/gather_blocks/all_to_all | solution.py:151
  73.7 4.3 %all-to-all-start.2 = ((bf16[96,128,128]{2,1,0:T(8,128)(2,1)}), bf16[96,128,128]{2,1,0:T(8,128)(2,1)S(1)}, u32[]{:S(2)}, u32[]{:S(2)}) async-start(bf16[96,128,128]{2,1,0:T(8,128)(2,1)} %copy-done.3), calls=%async_computation.3 | async-start | bytes 6291456 | tf_op jit(solution)/shard_map/sum_terms_x/all_to_all | solution.py:151
  78.1 1.2 copy-done.1
  79.4 1.0 copy-done.14
  80.4 4.8 %forward.1 = (bf16[32,128,128]{2,1,0:T(8,128)(2,1)S(1)}, bf16[32,128,128]{2,1,0:T(8,128)(2,1)S(1)}) custom-call(s32[96]{0:T(128)S(1)} %bitcast.16, s32[96]{0:T(128)S(1)} %bitcast.19, s32[2]{0:T(128)S(1)} %pad_add_fusion.me_ref, bf16[13,128,128]{2,1,0:T(8,128)(2,1)S(1)} %copy-done.14, bf16[16,128,128]{2,1,0:T(8,128)(2,1)} %all-to-all-done.refs_0_, ...), custom_call_target="tpu_custom_call" | custom-call | flops 1610612736 | bytes 6000000 | tf_op jit(solution)/shard_map/forward/pallas_call | solution.py:35
  85.2 1.9 %collective-permute-start.6 = (bf16[32,128,128]{2,1,0:T(8,128)(2,1)S(1)}, bf16[32,128,128]{2,1,0:T(8,128)(2,1)S(1)}, u32[]{:S(2)}, u32[]{:S(2)}) collective-permute-start(bf16[32,128,128]{2,1,0:T(8,128)(2,1)S(1)} %get-tuple-element.25), channel_id=1, source_target_pairs={{0,1},{1,0},{2,3},{3,2},{4,5},{5,4},{6,7},{7,6},{8,9},{9,8},{10,11... | collective-permute-start | bytes 3145736 | tf_op jit(solution)/shard_map/sum_output/ppermute | solution.py:187
  87.1 2.6 %collective-permute-done.6 = bf16[32,128,128]{2,1,0:T(8,128)(2,1)S(1)} collective-permute-done((bf16[32,128,128]{2,1,0:T(8,128)(2,1)S(1)}, bf16[32,128,128]{2,1,0:T(8,128)(2,1)S(1)}, u32[]{:S(2)}, u32[]{:S(2)}) %collective-permute-start.6) | collective-permute-done | bytes 1048608 | tf_op jit(solution)/shard_map/sum_output/ppermute | solution.py:187
  89.7 1.5 add_convert_fusion
  91.2 1.2 copy-done.2
  92.4 1.6 %copy-done.6 = bf16[64,128,128]{2,1,0:T(8,128)(2,1)S(1)} copy-done((bf16[64,128,128]{2,1,0:T(8,128)(2,1)S(1)}, bf16[64,128,128]{2,1,0:T(8,128)(2,1)}, u32[]{:S(2)}) %copy-start.6) | copy-done | bytes 2097176
  94.0 1.0 copy-done.8
  96.1 6.6 %backward.1 = (bf16[128,1664]{1,0:T(8,128)(2,1)}, bf16[128,1664]{1,0:T(8,128)(2,1)}) custom-call(s32[96]{0:T(128)S(1)} %bitcast.17, s32[96]{0:T(128)S(1)} %bitcast.20, s32[2]{0:T(128)S(1)} %pad_add_fusion.me_ref, bf16[64,128,128]{2,1,0:T(8,128)(2,1)S(1)} %copy-done.6, bf16[128,1664]{1,0:T(8,128)(2,1)S(1)} %copy-done.8, bf16[128,1664]{1,0:T(8,128)(2,1)S(1)} %copy-done.10, ...), custom_call_target="tpu_custom_call" | custom-call | flops 1610612736 | bytes 8000000 | tf_op jit(solution)/shard_map/backward/pallas_call | solution.py:35
  102.7 13.1 %all-to-all-done.2.arrived_ref = bf16[96,128,128]{2,1,0:T(8,128)(2,1)S(1)} async-done(((bf16[96,128,128]{2,1,0:T(8,128)(2,1)}), bf16[96,128,128]{2,1,0:T(8,128)(2,1)S(1)}, u32[]{:S(2)}, u32[]{:S(2)}) %all-to-all-start.2) | async-done | bytes 3145760 | tf_op jit(solution)/shard_map/sum_terms_x/all_to_all | solution.py:151
  117.2 3.5 %all-to-all-start.3 = ((bf16[24,128,128]{2,1,0:T(8,128)(2,1)}), bf16[24,128,128]{2,1,0:T(8,128)(2,1)S(1)}, u32[]{:S(2)}, u32[]{:S(2)}) async-start(bf16[24,128,128]{2,1,0:T(8,128)(2,1)} %copy-done.4), calls=%async_computation.4 | async-start | bytes 1572864 | tf_op jit(solution)/shard_map/sum_terms_z/all_to_all | solution.py:151
  120.7 9.0 %reduce-scatter.2.cloned.1.call-done = bf16[4,128,128]{2,1,0:T(8,128)(2,1)} async-done(((bf16[32,128,128]{2,1,0:T(8,128)(2,1)}), bf16[4,128,128]{2,1,0:T(8,128)(2,1)}) %reduce-scatter.2.cloned.1.call-update) | async-done | bytes 131088 | tf_op jit(solution)/shard_map/sum_output/reduce_scatter | solution.py:190
  129.7 1.0 copy.18
  131.5 11.6 %all-to-all-done.3.arrived_ref = bf16[24,128,128]{2,1,0:T(8,128)(2,1)S(1)} async-done(((bf16[24,128,128]{2,1,0:T(8,128)(2,1)}), bf16[24,128,128]{2,1,0:T(8,128)(2,1)S(1)}, u32[]{:S(2)}, u32[]{:S(2)}) %all-to-all-start.3) | async-done | bytes 786464 | tf_op jit(solution)/shard_map/sum_terms_z/all_to_all | solution.py:151
  (43 shorter events, 8.8 us)
Async XLA Ops:
  7.2 48.3 %all-gather.2.cloned.1.call-start = ((), (), s32[]{:S(2)}) async-start(), calls=%async_computation.5 | async-start | bytes 2228224 | tf_op jit(solution)/shard_map/gather_out_grad/all_gather | solution.py:167
  10.8 44.3 %copy-start.7 = (bf16[128,1664]{1,0:T(8,128)(2,1)S(1)}, bf16[128,1664]{1,0:T(8,128)(2,1)}, u32[]{:S(2)}) copy-start(bf16[128,1664]{1,0:T(8,128)(2,1)} %gate_ref.3) | copy-start | bytes 1277956
  10.8 44.3 %copy-start.9 = (bf16[128,1664]{1,0:T(8,128)(2,1)S(1)}, bf16[128,1664]{1,0:T(8,128)(2,1)}, u32[]{:S(2)}) copy-start(bf16[128,1664]{1,0:T(8,128)(2,1)} %up_ref.3) | copy-start | bytes 1277956
  10.8 28.0 %all-to-all-start = ((bf16[16,128,128]{2,1,0:T(8,128)(2,1)}), bf16[16,128,128]{2,1,0:T(8,128)(2,1)}, u32[]{:S(2)}, u32[]{:S(2)}) async-start(bf16[16,128,128]{2,1,0:T(8,128)(2,1)} %bitcast.7), calls=%async_computation | async-start | bytes 1048576 | tf_op jit(solution)/shard_map/gather_blocks/all_to_all | solution.py:151
  22.0 11.4 %collective-permute-start.3 = (bf16[1,128,128]{2,1,0:T(8,128)(2,1)S(1)}, bf16[1,128,128]{2,1,0:T(8,128)(2,1)S(1)}, u32[]{:S(2)}, u32[]{:S(2)}) collective-permute-start(bf16[1,128,128]{2,1,0:T(8,128)(2,1)S(1)} %slice.7), channel_id=1, source_target_pairs={{0,16},{16,32},{32,48},{48,0},{64,80},{80,96},{96,112},{112,64},{1... | collective-permute-start | bytes 98312 | tf_op jit(solution)/shard_map/gather_blocks/ppermute | solution.py:171
  25.4 8.0 %collective-permute-start.4 = (bf16[1,128,128]{2,1,0:T(8,128)(2,1)S(1)}, bf16[1,128,128]{2,1,0:T(8,128)(2,1)S(1)}, u32[]{:S(2)}, u32[]{:S(2)}) collective-permute-start(bf16[1,128,128]{2,1,0:T(8,128)(2,1)S(1)} %slice.7), channel_id=1, source_target_pairs={{0,32},{16,48},{32,0},{48,16},{64,96},{80,112},{96,64},{112,80},{1... | collective-permute-start | bytes 98312 | tf_op jit(solution)/shard_map/gather_blocks/ppermute | solution.py:171
  30.0 5.8 %collective-permute-start.5 = (bf16[1,128,128]{2,1,0:T(8,128)(2,1)S(1)}, bf16[1,128,128]{2,1,0:T(8,128)(2,1)S(1)}, u32[]{:S(2)}, u32[]{:S(2)}) collective-permute-start(bf16[1,128,128]{2,1,0:T(8,128)(2,1)S(1)} %slice.7), channel_id=1, source_target_pairs={{0,48},{16,0},{32,16},{48,32},{64,112},{80,64},{96,80},{112,96},{1... | collective-permute-start | bytes 98312 | tf_op jit(solution)/shard_map/gather_blocks/ppermute | solution.py:171
  40.1 32.7 %all-to-all-start.1 = ((bf16[32,128,128]{2,1,0:T(8,128)(2,1)}), bf16[32,128,128]{2,1,0:T(8,128)(2,1)S(1)}, u32[]{:S(2)}, u32[]{:S(2)}) async-start(bf16[32,128,128]{2,1,0:T(8,128)(2,1)} %bitcast.8), calls=%async_computation.1 | async-start | bytes 2097152 | tf_op jit(solution)/shard_map/gather_blocks/all_to_all | solution.py:151
  44.3 11.2 %copy-start.11 = (s32[96,1]{0,1:T(1,128)S(1)}, s32[96,1]{0,1:T(1,128)}, u32[]{:S(2)}) copy-start(s32[96,1]{0,1:T(1,128)} %param.10) | copy-start | bytes 1156
  44.3 11.2 %copy-start.12 = (s32[96,1]{0,1:T(1,128)S(1)}, s32[96,1]{0,1:T(1,128)}, u32[]{:S(2)}) copy-start(s32[96,1]{0,1:T(1,128)} %param.11) | copy-start | bytes 1156
  44.3 33.8 %collective-permute-start = (bf16[16,128,128]{2,1,0:T(8,128)(2,1)}, bf16[16,128,128]{2,1,0:T(8,128)(2,1)}, u32[]{:S(2)}, u32[]{:S(2)}) collective-permute-start(bf16[16,128,128]{2,1,0:T(8,128)(2,1)} %all-to-all-done.refs_0_), channel_id=1, source_target_pairs={{0,16},{16,32},{32,48},{48,0},{64,80},{80,96},{96,112},{112,64},{1... | collective-permute-start | bytes 1572872 | tf_op jit(solution)/shard_map/gather_blocks/ppermute | solution.py:173
  47.1 31.1 %collective-permute-start.1 = (bf16[16,128,128]{2,1,0:T(8,128)(2,1)}, bf16[16,128,128]{2,1,0:T(8,128)(2,1)}, u32[]{:S(2)}, u32[]{:S(2)}) collective-permute-start(bf16[16,128,128]{2,1,0:T(8,128)(2,1)} %all-to-all-done.refs_0_), channel_id=1, source_target_pairs={{0,32},{16,48},{32,0},{48,16},{64,96},{80,112},{96,64},{112,80},{1... | collective-permute-start | bytes 1572872 | tf_op jit(solution)/shard_map/gather_blocks/ppermute | solution.py:173
  52.4 25.7 %collective-permute-start.2 = (bf16[16,128,128]{2,1,0:T(8,128)(2,1)}, bf16[16,128,128]{2,1,0:T(8,128)(2,1)}, u32[]{:S(2)}, u32[]{:S(2)}) collective-permute-start(bf16[16,128,128]{2,1,0:T(8,128)(2,1)} %all-to-all-done.refs_0_), channel_id=1, source_target_pairs={{0,48},{16,0},{32,16},{48,32},{64,112},{80,64},{96,80},{112,96},{1... | collective-permute-start | bytes 1572872 | tf_op jit(solution)/shard_map/gather_blocks/ppermute | solution.py:173
  55.4 5.4 %copy-start.13 = (bf16[13,128,128]{2,1,0:T(8,128)(2,1)}, bf16[13,128,128]{2,1,0:T(8,128)(2,1)S(1)}, u32[]{:S(2)}) copy-start(bf16[13,128,128]{2,1,0:T(8,128)(2,1)S(1)} %get-tuple-element.22.hid_ref) | copy-start | bytes 1277956
  55.5 1.7 %copy-start.5 = (bf16[64,128,128]{2,1,0:T(8,128)(2,1)S(1)}, bf16[64,128,128]{2,1,0:T(8,128)(2,1)}, u32[]{:S(2)}) copy-start(bf16[64,128,128]{2,1,0:T(8,128)(2,1)} %all-gather.2.cloned.1.call-done.grad_ref) | copy-start | bytes 6291460
  60.8 1.6 %copy-start.3 = (bf16[96,128,128]{2,1,0:T(8,128)(2,1)}, bf16[96,128,128]{2,1,0:T(8,128)(2,1)S(1)}, u32[]{:S(2)}) copy-start(bf16[96,128,128]{2,1,0:T(8,128)(2,1)S(1)} %terms.1) | copy-start | bytes 9437188
  72.7 1.0 copy-start
  73.7 42.1 %all-to-all-start.2 = ((bf16[96,128,128]{2,1,0:T(8,128)(2,1)}), bf16[96,128,128]{2,1,0:T(8,128)(2,1)S(1)}, u32[]{:S(2)}, u32[]{:S(2)}) async-start(bf16[96,128,128]{2,1,0:T(8,128)(2,1)} %copy-done.3), calls=%async_computation.3 | async-start | bytes 6291456 | tf_op jit(solution)/shard_map/sum_terms_x/all_to_all | solution.py:151
  78.0 51.7 %reduce-scatter.2.cloned.1.call-start = ((), (), s32[]{:S(2)}) async-start(), calls=%async_computation.6 | async-start | bytes 1179648 | tf_op jit(solution)/shard_map/sum_output/reduce_scatter | solution.py:190
  78.1 1.2 copy-start.1
  79.4 1.0 copy-start.14
  85.2 4.6 %collective-permute-start.6 = (bf16[32,128,128]{2,1,0:T(8,128)(2,1)S(1)}, bf16[32,128,128]{2,1,0:T(8,128)(2,1)S(1)}, u32[]{:S(2)}, u32[]{:S(2)}) collective-permute-start(bf16[32,128,128]{2,1,0:T(8,128)(2,1)S(1)} %get-tuple-element.25), channel_id=1, source_target_pairs={{0,1},{1,0},{2,3},{3,2},{4,5},{5,4},{6,7},{7,6},{8,9},{9,8},{10,11... | collective-permute-start | bytes 3145736 | tf_op jit(solution)/shard_map/sum_output/ppermute | solution.py:187
  91.2 1.2 copy-start.2
  92.4 1.6 %copy-start.6 = (bf16[64,128,128]{2,1,0:T(8,128)(2,1)S(1)}, bf16[64,128,128]{2,1,0:T(8,128)(2,1)}, u32[]{:S(2)}) copy-start(bf16[64,128,128]{2,1,0:T(8,128)(2,1)} %all-gather.2.cloned.1.call-done.grad_ref) | copy-start | bytes 6291460
  94.0 1.0 copy-start.8
  95.0 1.0 copy-start.10
  116.3 0.9 copy-start.4
  117.2 25.9 %all-to-all-start.3 = ((bf16[24,128,128]{2,1,0:T(8,128)(2,1)}), bf16[24,128,128]{2,1,0:T(8,128)(2,1)S(1)}, u32[]{:S(2)}, u32[]{:S(2)}) async-start(bf16[24,128,128]{2,1,0:T(8,128)(2,1)} %copy-done.4), calls=%async_computation.4 | async-start | bytes 1572864 | tf_op jit(solution)/shard_map/sum_terms_z/all_to_all | solution.py:151
Sparse Core Ops, SparseCore 0:
  10.7 44.7 all-gather.1
  91.3 38.3 reduce-scatter.1

commit v3 on v2

v3 whole, which is shorter than its diff:
```python
import functools

import jax
import jax.numpy as jnp
from jax import lax
from jax.experimental import pallas as pl
from jax.experimental.pallas import tpu as pltpu
from jax.sharding import PartitionSpec as P

BLK = 128
HID_TILES = 13
WIDTH_TILES = 64
GROUP_BLOCKS = 96
OWNED = 3
FAR = 2
NX, NY, NZ = 4, 8, 8
STEP = 16

SMEM = pl.BlockSpec(memory_space=pltpu.SMEM)
VMEM = pl.BlockSpec(memory_space=pltpu.VMEM)
HBM = pl.BlockSpec(memory_space=pltpu.HBM)


def x_shift(step):
    return [(z * NX + x, z * NX + (x + step) % NX) for z in range(NZ) for x in range(NX)]


CORE_SWAP = [(t, t ^ 1) for t in range(2 * NY)]
Z_GROUPS = [[z * NX + x for z in range(NZ)] for x in range(NX)]
X_GROUPS = [[z * NX + x for x in range(NX)] for z in range(NZ)]
NEAR, APART = 8, 4
NEAR_GROUPS = [[p * NEAR + q for q in range(NEAR)] for p in range(APART)]
APART_GROUPS = [[p * NEAR + q for p in range(APART)] for q in range(NEAR)]
Y_GROUPS = [[y * 2 + c for y in range(NY)] for c in range(2)]


def call(kernel, outs, index, far_ins, near_ins=(), scratch=(), out_spec=VMEM, flops=0, moved=0, vmem=60):
    n, m, k = len(index), len(far_ins), len(near_ins)
    count = len(jax.tree.leaves(outs))

    def body(*refs):
        far = refs[n:n + m]
        rest = refs[n + m:n + m + k + count + len(scratch)]
        buffers, sems = refs[len(refs) - m - 1:-1], refs[-1]
        copies = [pltpu.make_async_copy(src, dst, sems.at[i]) for i, (src, dst) in enumerate(zip(far, buffers))]
        for copy in copies:
            copy.start()

        def fetch(i):
            copies[i].wait()
            return buffers[i]
        kernel(fetch, *refs[:n], *rest)

    return pl.pallas_call(
        body,
        out_shape=outs,
        in_specs=[SMEM] * n + [HBM] * m + [VMEM] * k,
        out_specs=jax.tree.map(lambda _: out_spec, outs),
        scratch_shapes=[*scratch, *[pltpu.VMEM(a.shape, a.dtype) for a in far_ins], pltpu.SemaphoreType.DMA((max(m, 1),))],
        compiler_params=pltpu.CompilerParams(vmem_limit_bytes=vmem * 1024 * 1024),
        cost_estimate=pl.CostEstimate(flops=flops, bytes_accessed=moved, transcendentals=0),
    )(*index, *far_ins, *near_ins)


def tiles(n, dtype=jnp.bfloat16):
    return jax.ShapeDtypeStruct((n, BLK, BLK), dtype)


def block_of(z, x, place):
    return (z * NX + x) * OWNED + place


def far_at(a, i, me_x, sign):
    return block_of(i // FAR, lax.rem(me_x + sign * a + NX, NX), lax.rem(i, FAR))


def near_at(i):
    return block_of(i // NX, lax.rem(i, NX), FAR)


def each_block(fetch, first, me_x, visit):
    for a in range(NX + 1):
        ref = fetch(first + a)

        def some(g, carry, a=a, ref=ref):
            entries = [g * STEP + j for j in range(STEP)]
            visit(ref, [(i, far_at(a, i, me_x, -1) if a < NX else near_at(i)) for i in entries])
            return carry
        lax.fori_loop(0, ref.shape[0] // STEP, some, 0)


def prepare_kernel(fetch, grad_tiles_ref, far_ref, near_ref):
    grad_ref, blocks_ref = fetch(0), fetch(1)
    for t in range(4):
        grad_tiles_ref[t] = grad_ref[:, t * BLK:(t + 1) * BLK]
    for z in range(NZ):
        for j in range(FAR):
            far_ref[z * FAR + j] = blocks_ref[j]
    near_ref[...] = blocks_ref[FAR:]


def hidden_kernel(fetch, hid_ref, hid_t_ref):
    gate_ref, up_ref = fetch(0), fetch(1)
    for r in range(HID_TILES):
        here = slice(r * BLK, (r + 1) * BLK)
        gate = gate_ref[:, here].astype(jnp.float32)
        hidden = gate * jax.nn.sigmoid(gate) * up_ref[:, here].astype(jnp.float32)
        hid_ref[r] = hidden.astype(jnp.bfloat16)
        hid_t_ref[r] = hidden.T.astype(jnp.bfloat16)


def terms_kernel(fetch, rows_ref, cols_ref, out_ref, terms, sems):
    hid_t_ref, grad_ref = fetch(0), fetch(1)

    def leave(g):
        here = pl.ds(g * STEP, STEP)
        return pltpu.make_async_copy(terms.at[here], out_ref.at[here], sems.at[g])

    def some(g, carry):
        for j in range(STEP):
            i = g * STEP + j
            p, q = lax.rem(i // OWNED, APART), i // (APART * OWNED)
            k = (p * NEAR + q) * OWNED + lax.rem(i, OWNED)
            terms[i] = jnp.dot(
                hid_t_ref[rows_ref[k]], grad_ref[cols_ref[k]], preferred_element_type=jnp.float32
            ).astype(jnp.bfloat16)
        leave(g).start()
        return carry
    lax.fori_loop(0, GROUP_BLOCKS // STEP, some, 0)
    for g in range(GROUP_BLOCKS // STEP):
        leave(g).wait()


def forward_kernel(fetch, rows_ref, cols_ref, me_ref, keep_ref, send_ref, total):
    core = me_ref[1]
    total[...] = jnp.zeros_like(total)
    hid_ref = fetch(0)

    def visit(ref, entries):
        found = [
            (cols_ref[k], jnp.dot(hid_ref[rows_ref[k]], ref[i], preferred_element_type=jnp.float32)) for i, k in entries
        ]
        for c, value in found:
            total[c] += value
    each_block(fetch, 1, me_ref[0], visit)

    def put(y, carry):
        mine, other = (y * 2 + core) * 4, (y * 2 + 1 - core) * 4
        for j in range(4):
            keep_ref[y * 4 + j] = total[mine + j].astype(jnp.bfloat16)
            send_ref[y * 4 + j] = total[other + j].astype(jnp.bfloat16)
        return carry
    lax.fori_loop(0, NY, put, 0)


def backward_kernel(fetch, rows_ref, cols_ref, me_ref, d_gate_ref, d_up_ref, total):
    total[...] = jnp.zeros_like(total)
    grad_ref, gate_ref, up_ref = fetch(0), fetch(1), fetch(2)

    def visit(ref, entries):
        found = [
            (rows_ref[k], lax.dot_general(
                grad_ref[cols_ref[k]], ref[i], (((1,), (1,)), ((), ())), preferred_element_type=jnp.float32
            )) for i, k in entries
        ]
        for r, value in found:
            total[r] += value
    each_block(fetch, 3, me_ref[0], visit)
    for r in range(HID_TILES):
        here = slice(r * BLK, (r + 1) * BLK)
        gate = gate_ref[:, here].astype(jnp.float32)
        up = up_ref[:, here].astype(jnp.float32)
        sigma = jax.nn.sigmoid(gate)
        back = total[r]
        d_gate_ref[:, here] = (back * up * sigma * (1.0 + gate * (1.0 - sigma))).astype(jnp.bfloat16)
        d_up_ref[:, here] = (back * gate * sigma).astype(jnp.bfloat16)


def pair_kernel(fetch, keep_ref, swapped_ref, out_ref, pair, sems):
    def leave(g):
        here = pl.ds(g * 8, 8)
        return pltpu.make_async_copy(pair.at[here], out_ref.at[here], sems.at[g])

    for g in range(4):
        here = pl.ds(g * 8, 8)
        pair[here] = (keep_ref[here].astype(jnp.float32) + swapped_ref[here].astype(jnp.float32)).astype(jnp.bfloat16)
        leave(g).start()
    for g in range(4):
        leave(g).wait()


def output_kernel(fetch, out_ref):
    tiles_ref = fetch(0)
    for t in range(4):
        out_ref[:, t * BLK:(t + 1) * BLK] = tiles_ref[t]


def sum_kernel(parts, fetch, arrived_ref, out_ref):
    n = out_ref.shape[0]
    for j in range(n):
        total = arrived_ref[j].astype(jnp.float32)
        for p in range(1, parts):
            total += arrived_ref[p * n + j].astype(jnp.float32)
        out_ref[j] = total.astype(out_ref.dtype)


def exchange(a, groups):
    return lax.all_to_all(a, "fsdp", 0, 0, tiled=True, axis_index_groups=groups)


def to_all(a):
    return jnp.broadcast_to(a[None], (NZ, *a.shape)).reshape(NZ * a.shape[0], BLK, BLK)


def shards(gate_pre, up_pre, out_grad, down_blocks, block_rows, block_cols):
    rows, cols = block_rows[:, 0], block_cols[:, 0]
    me = jnp.stack([lax.rem(lax.axis_index("fsdp"), NX), lax.rem(lax.axis_index("tensor"), 2)]).astype(jnp.int32)
    macs = GROUP_BLOCKS * BLK**3
    blocks = down_blocks.reshape(OWNED, BLK, BLK)

    with jax.named_scope("gather_out_grad"):
        grad_tiles, far, near = call(
            prepare_kernel, (tiles(4), tiles(NZ * FAR), tiles(OWNED - FAR)), (), (out_grad, blocks), moved=10**6
        )
        grad_tiles = lax.all_gather(grad_tiles, "tensor", axis=0, tiled=True)
    with jax.named_scope("gather_blocks"):
        far = exchange(far, Z_GROUPS)
        near = lax.all_gather(near, "fsdp", axis=0, axis_index_groups=X_GROUPS, tiled=True)
        near = exchange(to_all(near), Z_GROUPS)
        parts = [far] + [lax.ppermute(far, "fsdp", x_shift(s)) for s in range(1, NX)] + [near]
    with jax.named_scope("hidden"):
        hid, hid_t = call(hidden_kernel, (tiles(HID_TILES), tiles(HID_TILES)), (), (gate_pre, up_pre), flops=10**9, moved=4 * 10**6)
    with jax.named_scope("terms"):
        terms = call(
            terms_kernel, tiles(GROUP_BLOCKS), (rows, cols), (hid_t, grad_tiles), out_spec=HBM,
            scratch=[pltpu.VMEM((GROUP_BLOCKS, BLK, BLK), jnp.bfloat16), pltpu.SemaphoreType.DMA((GROUP_BLOCKS // STEP,))],
            flops=8 * macs, moved=6 * 10**6,
        )
        terms, hid = lax.optimization_barrier((terms, hid))
    with jax.named_scope("sum_terms_near"):
        terms, parts = lax.optimization_barrier((terms, parts))
        terms = exchange(terms, NEAR_GROUPS)
    with jax.named_scope("forward"):
        keep, send = call(
            forward_kernel, (tiles(32), tiles(32)), (rows, cols, me), (hid, *parts),
            scratch=[pltpu.VMEM((WIDTH_TILES, BLK, BLK), jnp.float32)], flops=8 * macs, moved=6 * 10**6, vmem=60,
        )
    with jax.named_scope("sum_output"):
        swapped = lax.ppermute(send, "tensor", CORE_SWAP)
        pair = call(
            pair_kernel, tiles(32), (), (), (keep, swapped), out_spec=HBM,
            scratch=[pltpu.VMEM((32, BLK, BLK), jnp.bfloat16), pltpu.SemaphoreType.DMA((4,))], moved=3 * 10**6, vmem=60,
        )
        pair, me_late = lax.optimization_barrier((pair, me))
        output = lax.psum_scatter(pair, "tensor", scatter_dimension=0, axis_index_groups=Y_GROUPS, tiled=True)
        output = call(output_kernel, jax.ShapeDtypeStruct(out_grad.shape, jnp.bfloat16), (), (output,), moved=10**5)
    with jax.named_scope("backward"):
        wide = jax.ShapeDtypeStruct(gate_pre.shape, jnp.bfloat16)
        d_gate, d_up = call(
            backward_kernel, (wide, wide), (rows, cols, me_late), (grad_tiles, gate_pre, up_pre, *parts),
            scratch=[pltpu.VMEM((HID_TILES, BLK, BLK), jnp.float32)], flops=8 * macs, moved=8 * 10**6, vmem=60,
        )
    with jax.named_scope("sum_terms_apart"):
        terms, d_gate, d_up = lax.optimization_barrier((terms, d_gate, d_up))
        terms = call(functools.partial(sum_kernel, NEAR), tiles(APART * OWNED), (), (), (terms,), moved=4 * 10**6, vmem=24)
        terms = exchange(terms, APART_GROUPS)
        grad_blocks = call(functools.partial(sum_kernel, APART), tiles(OWNED, jnp.float32), (), (), (terms,), moved=10**6, vmem=24)
        grad_blocks = grad_blocks.reshape(OWNED, 1, BLK, BLK)
    return (output, d_gate, d_up, grad_blocks)


def solution(mesh):
    both = P("fsdp", "tensor")
    blocks = P("fsdp", "tensor", None, None)
    index = P(None, "tensor")
    return jax.shard_map(
        shards, mesh=mesh, in_specs=(both, both, both, blocks, index, index),
        out_specs=(both, both, both, blocks), check_vma=False,
    )
```

time: 153 us -> 145 us (0.948)
  local copies, waits for them, and re-layouts: 19.5 us -> 2.37 us
  blocking collectives: 0 us -> 12.5 us
  Pallas kernels: 16.6 us -> 27.9 us
  starting transfers between devices: 46.6 us -> 38.4 us
  waiting for transfers between devices: 52.1 us -> 48 us
    all_to_all x4, waiting for transfers between devices: 38 us -> 24.2 us  [exchange(): return lax.all_to_all(a, 'fsdp', 0, 0, tiled=True, axis_index_groups=groups)]
    unnamed x32 -> x10, local copies, waits for them, and re-layouts: 14 us -> 1.15 us
    all_gather x0 -> x1, blocking collectives: none -> 12.5 us  [shards(): lax.all_gather(near, 'fsdp', axis=0, axis_index_groups=X_GROUPS, tiled=True)]
    ppermute x3, waiting for transfers between devices: 0.01 us -> 11.4 us  [shards(): lax.ppermute(far, 'fsdp', x_shift(s))]
    ppermute x3 -> x0, starting transfers between devices: 11.4 us -> none  [shards(): lax.ppermute(near, 'fsdp', x_shift(s))]
    pallas_call x6 -> x9, Pallas kernels: 16.6 us -> 27.9 us  [call(): pl.pallas_call(body, out_shape=outs, in_specs=[SMEM] * n + [HBM] * m + [V...]
    all_to_all x4, starting transfers between devices: 22.6 us -> 25 us  [exchange(): return lax.all_to_all(a, 'fsdp', 0, 0, tiled=True, axis_index_groups=groups)]
    ppermute x3 -> x0, waiting for transfers between devices: 2.44 us -> none  [shards(): lax.ppermute(near, 'fsdp', x_shift(s))]
  transfers between devices with their start and end apart: 13 -> 10, of which waited for: 8 -> 8; matrix products, arithmetic and copies ran while one was open for 5% -> 1% of each run, Pallas kernels for 11% -> 18%
where the time goes in v3:
time: 145 us; the launch traced here: 144 us
  waiting for transfers between devices  48 us (33%)
  starting transfers between devices  38.4 us (26%)
  Pallas kernels  27.9 us (19%)
  between operations  14.2 us (10%)
  blocking collectives  12.5 us (9%)
  local copies, waits for them, and re-layouts  2.37 us (2%)
    pallas_call x9, Pallas kernels, call(): pl.pallas_call(body, out_shape=outs, in_specs=[SMEM] * n + [HBM] * m + [V...  27.9 us
    all_to_all x4, starting transfers between devices, exchange(): return lax.all_to_all(a, 'fsdp', 0, 0, tiled=True, axis_index_groups=groups)  25 us
    all_to_all x4, waiting for transfers between devices, exchange(): return lax.all_to_all(a, 'fsdp', 0, 0, tiled=True, axis_index_groups=groups)  24.2 us
    all_gather x1, blocking collectives, shards(): lax.all_gather(near, 'fsdp', axis=0, axis_index_groups=X_GROUPS, tiled=True)  12.5 us
    ppermute x3, waiting for transfers between devices, shards(): lax.ppermute(far, 'fsdp', x_shift(s))  11.4 us
    ppermute x3, starting transfers between devices, shards(): lax.ppermute(far, 'fsdp', x_shift(s))  11.4 us
    reduce_scatter x1, waiting for transfers between devices, shards(): lax.psum_scatter(pair, 'tensor', scatter_dimension=0, axis_index_groups=Y...  9.19 us
    ppermute x1, waiting for transfers between devices, shards(): swapped = lax.ppermute(send, 'tensor', CORE_SWAP)  2.97 us
  transfers between devices with their start and end apart: 10, of which 8 were waited for; matrix products, arithmetic and copies ran while one was open for 1% of the time, Pallas kernels for 18%

profile of v3, /device:TPU:56, one launch (start us, length us, event | category | flops | bytes accessed | tf_op | source)
XLA Modules:
  0.0 144.0 jit_solution(7463792038228268102)
XLA Ops:
  7.2 0.0 all-gather.2.cloned.1.call-start
  7.2 1.9 %gather_out_grad.1 = (bf16[4,128,128]{2,1,0:T(8,128)(2,1)}, bf16[16,128,128]{2,1,0:T(8,128)(2,1)}, bf16[1,128,128]{2,1,0:T(8,128)(2,1)}) custom-call(bf16[128,512]{1,0:T(8,128)(2,1)} %refs_0_.3, bf16[3,128,128]{2,1,0:T(8,128)(2,1)} %bitcast.10), custom_call_target="tpu_custom_call" | custom-call | bytes 1000000 | tf_op jit(solution)/shard_map/gather_out_grad/pallas_call | solution.py:54
  9.1 10.3 %all-to-all-start = ((bf16[16,128,128]{2,1,0:T(8,128)(2,1)}), bf16[16,128,128]{2,1,0:T(8,128)(2,1)S(1)}, u32[]{:S(2)}, u32[]{:S(2)}) async-start(bf16[16,128,128]{2,1,0:T(8,128)(2,1)} %get-tuple-element.31), calls=%async_computation | async-start | bytes 1048576 | tf_op jit(solution)/shard_map/gather_blocks/all_to_all | solution.py:208
  19.4 12.5 %all_gather.7 = bf16[4,128,128]{2,1,0:T(8,128)(2,1)S(1)} all-gather(bf16[1,128,128]{2,1,0:T(8,128)(2,1)} %get-tuple-element.32), channel_id=1, replica_groups={{0,16,32,48},{64,80,96,112},{128,144,160,176},{192,208,224,240},{256,27..., dimensions={0}, use_global_device_ids=true | all-gather | bytes 163840 | tf_op jit(solution)/shard_map/gather_blocks/all_gather | solution.py:228
  32.0 5.0 %all-to-all-done.refs_4_.refs_6_ = bf16[16,128,128]{2,1,0:T(8,128)(2,1)S(1)} async-done(((bf16[16,128,128]{2,1,0:T(8,128)(2,1)}), bf16[16,128,128]{2,1,0:T(8,128)(2,1)S(1)}, u32[]{:S(2)}, u32[]{:S(2)}) %all-to-all-start) | async-done | bytes 524320 | tf_op jit(solution)/shard_map/gather_blocks/all_to_all | solution.py:208
  36.9 1.2 broadcast_in_dim.2
  38.2 3.6 %all-to-all-start.1 = ((bf16[32,128,128]{2,1,0:T(8,128)(2,1)}), bf16[32,128,128]{2,1,0:T(8,128)(2,1)S(1)}, u32[]{:S(2)}, u32[]{:S(2)}) async-start(bf16[32,128,128]{2,1,0:T(8,128)(2,1)} %bitcast.5), calls=%async_computation.1 | async-start | bytes 2097152 | tf_op jit(solution)/shard_map/gather_blocks/all_to_all | solution.py:208
  41.7 3.4 %collective-permute-start = (bf16[16,128,128]{2,1,0:T(8,128)(2,1)S(1)}, bf16[16,128,128]{2,1,0:T(8,128)(2,1)S(1)}, u32[]{:S(2)}, u32[]{:S(2)}) collective-permute-start(bf16[16,128,128]{2,1,0:T(8,128)(2,1)S(1)} %all-to-all-done.refs_4_.refs_6_), channel_id=1, source_target_pairs={{0,16},{16,32},{32,48},{48,0},{64,80},{80,96},{96,112},{112,64},{1... | collective-permute-start | bytes 1572872 | tf_op jit(solution)/shard_map/gather_blocks/ppermute | solution.py:230
  45.1 4.6 %collective-permute-start.1 = (bf16[16,128,128]{2,1,0:T(8,128)(2,1)S(1)}, bf16[16,128,128]{2,1,0:T(8,128)(2,1)S(1)}, u32[]{:S(2)}, u32[]{:S(2)}) collective-permute-start(bf16[16,128,128]{2,1,0:T(8,128)(2,1)S(1)} %all-to-all-done.refs_4_.refs_6_), channel_id=1, source_target_pairs={{0,32},{16,48},{32,0},{48,16},{64,96},{80,112},{96,64},{112,80},{1... | collective-permute-start | bytes 1572872 | tf_op jit(solution)/shard_map/gather_blocks/ppermute | solution.py:230
  49.8 3.3 %collective-permute-start.2 = (bf16[16,128,128]{2,1,0:T(8,128)(2,1)S(1)}, bf16[16,128,128]{2,1,0:T(8,128)(2,1)S(1)}, u32[]{:S(2)}, u32[]{:S(2)}) collective-permute-start(bf16[16,128,128]{2,1,0:T(8,128)(2,1)S(1)} %all-to-all-done.refs_4_.refs_6_), channel_id=1, source_target_pairs={{0,48},{16,0},{32,16},{48,32},{64,112},{80,64},{96,80},{112,96},{1... | collective-permute-start | bytes 1572872 | tf_op jit(solution)/shard_map/gather_blocks/ppermute | solution.py:230
  53.1 2.3 %hidden.1 = (bf16[13,128,128]{2,1,0:T(8,128)(2,1)}, bf16[13,128,128]{2,1,0:T(8,128)(2,1)}) custom-call(bf16[128,1664]{1,0:T(8,128)(2,1)} %refs_4_.1, bf16[128,1664]{1,0:T(8,128)(2,1)} %refs_5_.1), custom_call_target="tpu_custom_call" | custom-call | flops 1000000000 | bytes 4000000 | tf_op jit(solution)/shard_map/hidden/pallas_call | solution.py:54
  55.4 0.1 all-gather.2.cloned.1.call-done.refs_3_
  55.6 5.5 %terms.1 = bf16[96,128,128]{2,1,0:T(8,128)(2,1)} custom-call(s32[96]{0:T(128)} %bitcast.11, s32[96]{0:T(128)} %bitcast.14, bf16[13,128,128]{2,1,0:T(8,128)(2,1)} %get-tuple-element.26.refs_2_, bf16[64,128,128]{2,1,0:T(8,128)(2,1)} %all-gather.2.cloned.1.call-done.refs_3_), custom_call_target="tpu_custom_call" | custom-call | flops 1610612736 | bytes 6000000 | tf_op jit(solution)/shard_map/terms/pallas_call | solution.py:54
  61.0 9.9 %collective-permute-done.1.refs_6_.refs_8_ = bf16[16,128,128]{2,1,0:T(8,128)(2,1)S(1)} collective-permute-done((bf16[16,128,128]{2,1,0:T(8,128)(2,1)S(1)}, bf16[16,128,128]{2,1,0:T(8,128)(2,1)S(1)}, u32[]{:S(2)}, u32[]{:S(2)}) %collective-permute-start.1) | collective-permute-done | bytes 524320 | tf_op jit(solution)/shard_map/gather_blocks/ppermute | solution.py:230
  70.9 1.6 %collective-permute-done.2.refs_7_.refs_9_ = bf16[16,128,128]{2,1,0:T(8,128)(2,1)S(1)} collective-permute-done((bf16[16,128,128]{2,1,0:T(8,128)(2,1)S(1)}, bf16[16,128,128]{2,1,0:T(8,128)(2,1)S(1)}, u32[]{:S(2)}, u32[]{:S(2)}) %collective-permute-start.2) | collective-permute-done | bytes 524320 | tf_op jit(solution)/shard_map/gather_blocks/ppermute | solution.py:230
  72.5 0.8 copy-done.4
  73.3 0.4 copy-done
  73.6 5.4 %all-to-all-start.2 = ((bf16[96,128,128]{2,1,0:T(8,128)(2,1)}), bf16[96,128,128]{2,1,0:T(8,128)(2,1)S(1)}, u32[]{:S(2)}, u32[]{:S(2)}) async-start(bf16[96,128,128]{2,1,0:T(8,128)(2,1)} %terms.1), calls=%async_computation.3 | async-start | bytes 6291456 | tf_op jit(solution)/shard_map/sum_terms_near/all_to_all | solution.py:208
  79.0 0.0 reduce-scatter.2.cloned.1.call-start
  79.0 0.6 pad_add_fusion.refs_2_
  79.6 5.3 %forward.1 = (bf16[32,128,128]{2,1,0:T(8,128)(2,1)}, bf16[32,128,128]{2,1,0:T(8,128)(2,1)}) custom-call(s32[96]{0:T(128)} %bitcast.12, s32[96]{0:T(128)} %bitcast.15, s32[2]{0:T(128)} %pad_add_fusion.refs_2_, bf16[13,128,128]{2,1,0:T(8,128)(2,1)} %get-tuple-element.29.refs_3_, bf16[16,128,128]{2,1,0:T(8,128)(2,1)} %copy-done.1, ...), custom_call_target="tpu_custom_call" | custom-call | flops 1610612736 | bytes 6000000 | tf_op jit(solution)/shard_map/forward/pallas_call | solution.py:54
  84.9 1.9 %collective-permute-start.3 = (bf16[32,128,128]{2,1,0:T(8,128)(2,1)}, bf16[32,128,128]{2,1,0:T(8,128)(2,1)}, u32[]{:S(2)}, u32[]{:S(2)}) collective-permute-start(bf16[32,128,128]{2,1,0:T(8,128)(2,1)} %get-tuple-element.39), channel_id=1, source_target_pairs={{0,1},{1,0},{2,3},{3,2},{4,5},{5,4},{6,7},{7,6},{8,9},{9,8},{10,11... | collective-permute-start | bytes 3145736 | tf_op jit(solution)/shard_map/sum_output/ppermute | solution.py:249
  86.9 3.0 %collective-permute-done.3.refs_1_ = bf16[32,128,128]{2,1,0:T(8,128)(2,1)} collective-permute-done((bf16[32,128,128]{2,1,0:T(8,128)(2,1)}, bf16[32,128,128]{2,1,0:T(8,128)(2,1)}, u32[]{:S(2)}, u32[]{:S(2)}) %collective-permute-start.3) | collective-permute-done | bytes 1048608 | tf_op jit(solution)/shard_map/sum_output/ppermute | solution.py:249
  89.8 2.6 %sum_output.2 = bf16[32,128,128]{2,1,0:T(8,128)(2,1)} custom-call(bf16[32,128,128]{2,1,0:T(8,128)(2,1)} %get-tuple-element.38.refs_0_, bf16[32,128,128]{2,1,0:T(8,128)(2,1)} %collective-permute-done.3.refs_1_), custom_call_target="tpu_custom_call" | custom-call | bytes 3000000 | tf_op jit(solution)/shard_map/sum_output/pallas_call | solution.py:54
  92.5 7.0 %backward.1 = (bf16[128,1664]{1,0:T(8,128)(2,1)}, bf16[128,1664]{1,0:T(8,128)(2,1)}) custom-call(s32[96]{0:T(128)} %bitcast.13, s32[96]{0:T(128)} %bitcast.16, s32[2]{0:T(128)} %pad_add_fusion.refs_2_, bf16[64,128,128]{2,1,0:T(8,128)(2,1)} %all-gather.2.cloned.1.call-done.refs_3_, bf16[128,1664]{1,0:T(8,128)(2,1)} %refs_4_.1, bf16[128,1664]{1,0:T(8,128)(2,1)} %refs_5_.1, ...), custom_call_target="tpu_custom_call" | custom-call | flops 1610612736 | bytes 8000000 | tf_op jit(solution)/shard_map/backward/pallas_call | solution.py:54
  99.5 16.6 %all-to-all-done.2.refs_0_ = bf16[96,128,128]{2,1,0:T(8,128)(2,1)S(1)} async-done(((bf16[96,128,128]{2,1,0:T(8,128)(2,1)}), bf16[96,128,128]{2,1,0:T(8,128)(2,1)S(1)}, u32[]{:S(2)}, u32[]{:S(2)}) %all-to-all-start.2) | async-done | bytes 3145760 | tf_op jit(solution)/shard_map/sum_terms_near/all_to_all | solution.py:208
  116.0 1.2 sum_terms_apart.2
  117.2 5.8 %all-to-all-start.3 = ((bf16[12,128,128]{2,1,0:T(8,128)(2,1)}), bf16[12,128,128]{2,1,0:T(8,128)(2,1)S(1)}, u32[]{:S(2)}, u32[]{:S(2)}) async-start(bf16[12,128,128]{2,1,0:T(8,128)(2,1)} %sum_terms_apart.2), calls=%async_computation.4 | async-start | bytes 786432 | tf_op jit(solution)/shard_map/sum_terms_apart/all_to_all | solution.py:208
  123.0 9.2 %reduce-scatter.2.cloned.1.call-done.refs_0_ = bf16[4,128,128]{2,1,0:T(8,128)(2,1)} async-done(((bf16[32,128,128]{2,1,0:T(8,128)(2,1)}), bf16[4,128,128]{2,1,0:T(8,128)(2,1)}) %reduce-scatter.2.cloned.1.call-update) | async-done | bytes 131088 | tf_op jit(solution)/shard_map/sum_output/reduce_scatter | solution.py:255
  132.2 1.6 %sum_output.3 = bf16[128,512]{1,0:T(8,128)(2,1)} custom-call(bf16[4,128,128]{2,1,0:T(8,128)(2,1)} %reduce-scatter.2.cloned.1.call-done.refs_0_), custom_call_target="tpu_custom_call" | custom-call | bytes 100000 | tf_op jit(solution)/shard_map/sum_output/pallas_call | solution.py:54
  133.8 2.7 %all-to-all-done.3.refs_0_ = bf16[12,128,128]{2,1,0:T(8,128)(2,1)S(1)} async-done(((bf16[12,128,128]{2,1,0:T(8,128)(2,1)}), bf16[12,128,128]{2,1,0:T(8,128)(2,1)S(1)}, u32[]{:S(2)}, u32[]{:S(2)}) %all-to-all-start.3) | async-done | bytes 393248 | tf_op jit(solution)/shard_map/sum_terms_apart/all_to_all | solution.py:208
  136.4 0.7 sum_terms_apart.3
  (12 shorter events, 0.1 us)
Async XLA Ops:
  7.2 48.4 %all-gather.2.cloned.1.call-start = ((), (), s32[]{:S(2)}) async-start(), calls=%async_computation.5 | async-start | bytes 2228224 | tf_op jit(solution)/shard_map/gather_out_grad/all_gather | solution.py:225
  9.1 27.8 %all-to-all-start = ((bf16[16,128,128]{2,1,0:T(8,128)(2,1)}), bf16[16,128,128]{2,1,0:T(8,128)(2,1)S(1)}, u32[]{:S(2)}, u32[]{:S(2)}) async-start(bf16[16,128,128]{2,1,0:T(8,128)(2,1)} %get-tuple-element.31), calls=%async_computation | async-start | bytes 1048576 | tf_op jit(solution)/shard_map/gather_blocks/all_to_all | solution.py:208
  36.9 18.5 %copy-start.1 = (bf16[16,128,128]{2,1,0:T(8,128)(2,1)}, bf16[16,128,128]{2,1,0:T(8,128)(2,1)S(1)}, u32[]{:S(2)}) copy-start(bf16[16,128,128]{2,1,0:T(8,128)(2,1)S(1)} %all-to-all-done.refs_4_.refs_6_) | copy-start | bytes 1572868
  38.2 34.3 %all-to-all-start.1 = ((bf16[32,128,128]{2,1,0:T(8,128)(2,1)}), bf16[32,128,128]{2,1,0:T(8,128)(2,1)S(1)}, u32[]{:S(2)}, u32[]{:S(2)}) async-start(bf16[32,128,128]{2,1,0:T(8,128)(2,1)} %bitcast.5), calls=%async_computation.1 | async-start | bytes 2097152 | tf_op jit(solution)/shard_map/gather_blocks/all_to_all | solution.py:208
  41.7 19.3 %collective-permute-start = (bf16[16,128,128]{2,1,0:T(8,128)(2,1)S(1)}, bf16[16,128,128]{2,1,0:T(8,128)(2,1)S(1)}, u32[]{:S(2)}, u32[]{:S(2)}) collective-permute-start(bf16[16,128,128]{2,1,0:T(8,128)(2,1)S(1)} %all-to-all-done.refs_4_.refs_6_), channel_id=1, source_target_pairs={{0,16},{16,32},{32,48},{48,0},{64,80},{80,96},{96,112},{112,64},{1... | collective-permute-start | bytes 1572872 | tf_op jit(solution)/shard_map/gather_blocks/ppermute | solution.py:230
  45.1 25.8 %collective-permute-start.1 = (bf16[16,128,128]{2,1,0:T(8,128)(2,1)S(1)}, bf16[16,128,128]{2,1,0:T(8,128)(2,1)S(1)}, u32[]{:S(2)}, u32[]{:S(2)}) collective-permute-start(bf16[16,128,128]{2,1,0:T(8,128)(2,1)S(1)} %all-to-all-done.refs_4_.refs_6_), channel_id=1, source_target_pairs={{0,32},{16,48},{32,0},{48,16},{64,96},{80,112},{96,64},{112,80},{1... | collective-permute-start | bytes 1572872 | tf_op jit(solution)/shard_map/gather_blocks/ppermute | solution.py:230
  49.8 22.7 %collective-permute-start.2 = (bf16[16,128,128]{2,1,0:T(8,128)(2,1)S(1)}, bf16[16,128,128]{2,1,0:T(8,128)(2,1)S(1)}, u32[]{:S(2)}, u32[]{:S(2)}) collective-permute-start(bf16[16,128,128]{2,1,0:T(8,128)(2,1)S(1)} %all-to-all-done.refs_4_.refs_6_), channel_id=1, source_target_pairs={{0,48},{16,0},{32,16},{48,32},{64,112},{80,64},{96,80},{112,96},{1... | collective-permute-start | bytes 1572872 | tf_op jit(solution)/shard_map/gather_blocks/ppermute | solution.py:230
  61.0 11.4 %copy-start.2 = (bf16[16,128,128]{2,1,0:T(8,128)(2,1)}, bf16[16,128,128]{2,1,0:T(8,128)(2,1)S(1)}, u32[]{:S(2)}) copy-start(bf16[16,128,128]{2,1,0:T(8,128)(2,1)S(1)} %collective-permute-done.refs_5_.refs_7_) | copy-start | bytes 1572868
  70.9 1.6 %copy-start.3 = (bf16[16,128,128]{2,1,0:T(8,128)(2,1)}, bf16[16,128,128]{2,1,0:T(8,128)(2,1)S(1)}, u32[]{:S(2)}) copy-start(bf16[16,128,128]{2,1,0:T(8,128)(2,1)S(1)} %collective-permute-done.1.refs_6_.refs_8_) | copy-start | bytes 1572868
  72.5 0.8 copy-start.4
  72.5 1.2 copy-start
  73.6 42.4 %all-to-all-start.2 = ((bf16[96,128,128]{2,1,0:T(8,128)(2,1)}), bf16[96,128,128]{2,1,0:T(8,128)(2,1)S(1)}, u32[]{:S(2)}, u32[]{:S(2)}) async-start(bf16[96,128,128]{2,1,0:T(8,128)(2,1)} %terms.1), calls=%async_computation.3 | async-start | bytes 6291456 | tf_op jit(solution)/shard_map/sum_terms_near/all_to_all | solution.py:208
  79.0 53.2 %reduce-scatter.2.cloned.1.call-start = ((), (), s32[]{:S(2)}) async-start(), calls=%async_computation.6 | async-start | bytes 1179648 | tf_op jit(solution)/shard_map/sum_output/reduce_scatter | solution.py:255
  84.9 4.9 %collective-permute-start.3 = (bf16[32,128,128]{2,1,0:T(8,128)(2,1)}, bf16[32,128,128]{2,1,0:T(8,128)(2,1)}, u32[]{:S(2)}, u32[]{:S(2)}) collective-permute-start(bf16[32,128,128]{2,1,0:T(8,128)(2,1)} %get-tuple-element.39), channel_id=1, source_target_pairs={{0,1},{1,0},{2,3},{3,2},{4,5},{5,4},{6,7},{7,6},{8,9},{9,8},{10,11... | collective-permute-start | bytes 3145736 | tf_op jit(solution)/shard_map/sum_output/ppermute | solution.py:249
  117.2 19.2 %all-to-all-start.3 = ((bf16[12,128,128]{2,1,0:T(8,128)(2,1)}), bf16[12,128,128]{2,1,0:T(8,128)(2,1)S(1)}, u32[]{:S(2)}, u32[]{:S(2)}) async-start(bf16[12,128,128]{2,1,0:T(8,128)(2,1)} %sum_terms_apart.2), calls=%async_computation.4 | async-start | bytes 786432 | tf_op jit(solution)/shard_map/sum_terms_apart/all_to_all | solution.py:208
Sparse Core Ops, SparseCore 0:
  10.7 44.8 all-gather.1
  92.6 39.5 reduce-scatter.1

commit v4 on v3

--- a/solution.py
+++ b/solution.py
@@ -34,7 +34,7 @@
 Y_GROUPS = [[y * 2 + c for y in range(NY)] for c in range(2)]
 
 
-def call(kernel, outs, index, far_ins, near_ins=(), scratch=(), out_spec=VMEM, flops=0, moved=0, vmem=60):
+def call(kernel, outs, index, far_ins, near_ins=(), scratch=(), out_spec=VMEM, near_spec=VMEM, flops=0, moved=0, vmem=60):
     n, m, k = len(index), len(far_ins), len(near_ins)
     count = len(jax.tree.leaves(outs))
 
@@ -54,7 +54,7 @@
     return pl.pallas_call(
         body,
         out_shape=outs,
-        in_specs=[SMEM] * n + [HBM] * m + [VMEM] * k,
+        in_specs=[SMEM] * n + [HBM] * m + [near_spec] * k,
         out_specs=jax.tree.map(lambda _: out_spec, outs),
         scratch_shapes=[*scratch, *[pltpu.VMEM(a.shape, a.dtype) for a in far_ins], pltpu.SemaphoreType.DMA((max(m, 1),))],
         compiler_params=pltpu.CompilerParams(vmem_limit_bytes=vmem * 1024 * 1024),
@@ -131,8 +131,8 @@
         leave(g).wait()
 
 
-def forward_kernel(fetch, rows_ref, cols_ref, me_ref, keep_ref, send_ref, total):
-    core = me_ref[1]
+def forward_kernel(fetch, rows_ref, cols_ref, keep_ref, send_ref, total, keep, send, sems):
+    me_x, core = lax.rem(lax.axis_index("fsdp"), NX), lax.rem(lax.axis_index("tensor"), 2)
     total[...] = jnp.zeros_like(total)
     hid_ref = fetch(0)
 
@@ -142,18 +142,30 @@
         ]
         for c, value in found:
             total[c] += value
-    each_block(fetch, 1, me_ref[0], visit)
+    each_block(fetch, 1, me_x, visit)
+
+    def leave(y):
+        here = pl.ds(y * 4, 4)
+        return [
+            pltpu.make_async_copy(src.at[here], dst.at[here], sems.at[i, y])
+            for i, (src, dst) in enumerate(((send, send_ref), (keep, keep_ref)))
+        ]
 
     def put(y, carry):
         mine, other = (y * 2 + core) * 4, (y * 2 + 1 - core) * 4
-        for j in range(4):
-            keep_ref[y * 4 + j] = total[mine + j].astype(jnp.bfloat16)
-            send_ref[y * 4 + j] = total[other + j].astype(jnp.bfloat16)
+        here = pl.ds(y * 4, 4)
+        send[here] = total[pl.ds(other, 4)].astype(jnp.bfloat16)
+        keep[here] = total[pl.ds(mine, 4)].astype(jnp.bfloat16)
+        for copy in leave(y):
+            copy.start()
         return carry
     lax.fori_loop(0, NY, put, 0)
-
-
-def backward_kernel(fetch, rows_ref, cols_ref, me_ref, d_gate_ref, d_up_ref, total):
+    for y in range(NY):
+        for copy in leave(y):
+            copy.wait()
+
+
+def backward_kernel(fetch, rows_ref, cols_ref, d_gate_ref, d_up_ref, total):
     total[...] = jnp.zeros_like(total)
     grad_ref, gate_ref, up_ref = fetch(0), fetch(1), fetch(2)
 
@@ -165,7 +177,7 @@
         ]
         for r, value in found:
             total[r] += value
-    each_block(fetch, 3, me_ref[0], visit)
+    each_block(fetch, 3, lax.rem(lax.axis_index("fsdp"), NX), visit)
     for r in range(HID_TILES):
         here = slice(r * BLK, (r + 1) * BLK)
         gate = gate_ref[:, here].astype(jnp.float32)
@@ -176,17 +188,23 @@
         d_up_ref[:, here] = (back * gate * sigma).astype(jnp.bfloat16)
 
 
-def pair_kernel(fetch, keep_ref, swapped_ref, out_ref, pair, sems):
-    def leave(g):
-        here = pl.ds(g * 8, 8)
-        return pltpu.make_async_copy(pair.at[here], out_ref.at[here], sems.at[g])
-
-    for g in range(4):
-        here = pl.ds(g * 8, 8)
-        pair[here] = (keep_ref[here].astype(jnp.float32) + swapped_ref[here].astype(jnp.float32)).astype(jnp.bfloat16)
-        leave(g).start()
-    for g in range(4):
-        leave(g).wait()
+def pair_kernel(fetch, keep_ref, swapped_ref, out_ref, keep, swapped, pair, sems):
+    parts = [pl.ds(g * 8, 8) for g in range(4)]
+    arrive = [
+        [pltpu.make_async_copy(src.at[here], dst.at[here], sems.at[i, g]) for i, (src, dst) in enumerate(((keep_ref, keep), (swapped_ref, swapped)))]
+        for g, here in enumerate(parts)
+    ]
+    leave = [pltpu.make_async_copy(pair.at[here], out_ref.at[here], sems.at[2, g]) for g, here in enumerate(parts)]
+    for copies in arrive:
+        for copy in copies:
+            copy.start()
+    for g, here in enumerate(parts):
+        for copy in arrive[g]:
+            copy.wait()
+        pair[here] = (keep[here].astype(jnp.float32) + swapped[here].astype(jnp.float32)).astype(jnp.bfloat16)
+        leave[g].start()
+    for copy in leave:
+        copy.wait()
 
 
 def output_kernel(fetch, out_ref):
@@ -214,7 +232,6 @@
 
 def shards(gate_pre, up_pre, out_grad, down_blocks, block_rows, block_cols):
     rows, cols = block_rows[:, 0], block_cols[:, 0]
-    me = jnp.stack([lax.rem(lax.axis_index("fsdp"), NX), lax.rem(lax.axis_index("tensor"), 2)]).astype(jnp.int32)
     macs = GROUP_BLOCKS * BLK**3
     blocks = down_blocks.reshape(OWNED, BLK, BLK)
 
@@ -238,26 +255,29 @@
         )
         terms, hid = lax.optimization_barrier((terms, hid))
     with jax.named_scope("sum_terms_near"):
-        terms, parts = lax.optimization_barrier((terms, parts))
         terms = exchange(terms, NEAR_GROUPS)
     with jax.named_scope("forward"):
         keep, send = call(
-            forward_kernel, (tiles(32), tiles(32)), (rows, cols, me), (hid, *parts),
-            scratch=[pltpu.VMEM((WIDTH_TILES, BLK, BLK), jnp.float32)], flops=8 * macs, moved=6 * 10**6, vmem=60,
+            forward_kernel, (tiles(32), tiles(32)), (rows, cols), (hid, *parts), out_spec=HBM,
+            scratch=[
+                pltpu.VMEM((WIDTH_TILES, BLK, BLK), jnp.float32), pltpu.VMEM((32, BLK, BLK), jnp.bfloat16),
+                pltpu.VMEM((32, BLK, BLK), jnp.bfloat16), pltpu.SemaphoreType.DMA((2, NY)),
+            ],
+            flops=200 * macs, moved=6 * 10**6,
         )
     with jax.named_scope("sum_output"):
         swapped = lax.ppermute(send, "tensor", CORE_SWAP)
         pair = call(
-            pair_kernel, tiles(32), (), (), (keep, swapped), out_spec=HBM,
-            scratch=[pltpu.VMEM((32, BLK, BLK), jnp.bfloat16), pltpu.SemaphoreType.DMA((4,))], moved=3 * 10**6, vmem=60,
-        )
-        pair, me_late = lax.optimization_barrier((pair, me))
+            pair_kernel, tiles(32), (), (), (keep, swapped), out_spec=HBM, near_spec=HBM,
+            scratch=[*[pltpu.VMEM((32, BLK, BLK), jnp.bfloat16)] * 3, pltpu.SemaphoreType.DMA((3, 4))], moved=3 * 10**6,
+        )
+        pair, rows_late = lax.optimization_barrier((pair, rows))
         output = lax.psum_scatter(pair, "tensor", scatter_dimension=0, axis_index_groups=Y_GROUPS, tiled=True)
         output = call(output_kernel, jax.ShapeDtypeStruct(out_grad.shape, jnp.bfloat16), (), (output,), moved=10**5)
     with jax.named_scope("backward"):
         wide = jax.ShapeDtypeStruct(gate_pre.shape, jnp.bfloat16)
         d_gate, d_up = call(
-            backward_kernel, (wide, wide), (rows, cols, me_late), (grad_tiles, gate_pre, up_pre, *parts),
+            backward_kernel, (wide, wide), (rows_late, cols), (grad_tiles, gate_pre, up_pre, *parts),
             scratch=[pltpu.VMEM((HID_TILES, BLK, BLK), jnp.float32)], flops=8 * macs, moved=8 * 10**6, vmem=60,
         )
     with jax.named_scope("sum_terms_apart"):

time: 145 us -> 140 us (0.966)
  starting transfers between devices: 38.4 us -> 35 us
    all_to_all x4, waiting for transfers between devices: 24.2 us -> 37.4 us  [exchange(): return lax.all_to_all(a, 'fsdp', 0, 0, tiled=True, axis_index_groups=groups)]
    ppermute x3, waiting for transfers between devices: 11.4 us -> 0.01 us  [shards(): lax.ppermute(far, 'fsdp', x_shift(s))]
    all_to_all x4, starting transfers between devices: 25 us -> 21.7 us  [exchange(): return lax.all_to_all(a, 'fsdp', 0, 0, tiled=True, axis_index_groups=groups)]
    reduce_scatter x1, waiting for transfers between devices: 9.19 us -> 7.23 us  [shards(): lax.psum_scatter(pair, 'tensor', scatter_dimension=0, axis_index_groups=Y...]
  transfers between devices with their start and end apart: 10 -> 10, of which waited for: 8 -> 7; matrix products, arithmetic and copies ran while one was open for 1% -> 1% of each run, Pallas kernels for 18% -> 18%
where the time goes in v4:
time: 140 us; the launch traced here: 139 us
  waiting for transfers between devices  47.7 us (34%)
  starting transfers between devices  35 us (25%)
  Pallas kernels  27.6 us (20%)
  between operations  14.2 us (10%)
  blocking collectives  12.5 us (9%)
  local copies, waits for them, and re-layouts  2.25 us (2%)
    all_to_all x4, waiting for transfers between devices, exchange(): return lax.all_to_all(a, 'fsdp', 0, 0, tiled=True, axis_index_groups=groups)  37.4 us
    pallas_call x9, Pallas kernels, call(): pl.pallas_call(body, out_shape=outs, in_specs=[SMEM] * n + [HBM] * m + [n...  27.6 us
    all_to_all x4, starting transfers between devices, exchange(): return lax.all_to_all(a, 'fsdp', 0, 0, tiled=True, axis_index_groups=groups)  21.7 us
    all_gather x1, blocking collectives, shards(): lax.all_gather(near, 'fsdp', axis=0, axis_index_groups=X_GROUPS, tiled=True)  12.5 us
    ppermute x3, starting transfers between devices, shards(): lax.ppermute(far, 'fsdp', x_shift(s))  11.4 us
    reduce_scatter x1, waiting for transfers between devices, shards(): lax.psum_scatter(pair, 'tensor', scatter_dimension=0, axis_index_groups=Y...  7.23 us
    ppermute x1, waiting for transfers between devices, shards(): swapped = lax.ppermute(send, 'tensor', CORE_SWAP)  2.97 us
  transfers between devices with their start and end apart: 10, of which 7 were waited for; matrix products, arithmetic and copies ran while one was open for 1% of the time, Pallas kernels for 18%

profile of v4, /device:TPU:56, one launch (start us, length us, event | category | flops | bytes accessed | tf_op | source)
XLA Modules:
  0.0 139.3 jit_solution(12167110199933677792)
XLA Ops:
  7.2 0.0 all-gather.2.cloned.1.call-start
  7.2 1.9 %gather_out_grad.1 = (bf16[4,128,128]{2,1,0:T(8,128)(2,1)}, bf16[16,128,128]{2,1,0:T(8,128)(2,1)}, bf16[1,128,128]{2,1,0:T(8,128)(2,1)}) custom-call(bf16[128,512]{1,0:T(8,128)(2,1)} %refs_0_.3, bf16[3,128,128]{2,1,0:T(8,128)(2,1)} %bitcast.8), custom_call_target="tpu_custom_call" | custom-call | bytes 1000000 | tf_op jit(solution)/shard_map/gather_out_grad/pallas_call | solution.py:54
  9.1 0.0 all-gather.2.cloned.1.call-update
  9.1 10.3 %all-to-all-start = ((bf16[16,128,128]{2,1,0:T(8,128)(2,1)}), bf16[16,128,128]{2,1,0:T(8,128)(2,1)}, u32[]{:S(2)}, u32[]{:S(2)}) async-start(bf16[16,128,128]{2,1,0:T(8,128)(2,1)} %get-tuple-element.24), calls=%async_computation | async-start | bytes 1048576 | tf_op jit(solution)/shard_map/gather_blocks/all_to_all | solution.py:226
  19.4 12.5 %all_gather.7 = bf16[4,128,128]{2,1,0:T(8,128)(2,1)S(1)} all-gather(bf16[1,128,128]{2,1,0:T(8,128)(2,1)} %get-tuple-element.25), channel_id=1, replica_groups={{0,16,32,48},{64,80,96,112},{128,144,160,176},{192,208,224,240},{256,27..., dimensions={0}, use_global_device_ids=true | all-gather | bytes 163840 | tf_op jit(solution)/shard_map/gather_blocks/all_gather | solution.py:245
  32.0 5.1 %all-to-all-done.refs_3_.refs_5_ = bf16[16,128,128]{2,1,0:T(8,128)(2,1)} async-done(((bf16[16,128,128]{2,1,0:T(8,128)(2,1)}), bf16[16,128,128]{2,1,0:T(8,128)(2,1)}, u32[]{:S(2)}, u32[]{:S(2)}) %all-to-all-start) | async-done | bytes 524320 | tf_op jit(solution)/shard_map/gather_blocks/all_to_all | solution.py:226
  37.0 1.2 broadcast_in_dim.2
  38.3 3.6 %all-to-all-start.1 = ((bf16[32,128,128]{2,1,0:T(8,128)(2,1)}), bf16[32,128,128]{2,1,0:T(8,128)(2,1)S(1)}, u32[]{:S(2)}, u32[]{:S(2)}) async-start(bf16[32,128,128]{2,1,0:T(8,128)(2,1)} %bitcast.3), calls=%async_computation.1 | async-start | bytes 2097152 | tf_op jit(solution)/shard_map/gather_blocks/all_to_all | solution.py:226
  41.9 3.4 %collective-permute-start = (bf16[16,128,128]{2,1,0:T(8,128)(2,1)}, bf16[16,128,128]{2,1,0:T(8,128)(2,1)}, u32[]{:S(2)}, u32[]{:S(2)}) collective-permute-start(bf16[16,128,128]{2,1,0:T(8,128)(2,1)} %all-to-all-done.refs_3_.refs_5_), channel_id=1, source_target_pairs={{0,16},{16,32},{32,48},{48,0},{64,80},{80,96},{96,112},{112,64},{1... | collective-permute-start | bytes 1572872 | tf_op jit(solution)/shard_map/gather_blocks/ppermute | solution.py:247
  45.3 4.6 %collective-permute-start.1 = (bf16[16,128,128]{2,1,0:T(8,128)(2,1)}, bf16[16,128,128]{2,1,0:T(8,128)(2,1)}, u32[]{:S(2)}, u32[]{:S(2)}) collective-permute-start(bf16[16,128,128]{2,1,0:T(8,128)(2,1)} %all-to-all-done.refs_3_.refs_5_), channel_id=1, source_target_pairs={{0,32},{16,48},{32,0},{48,16},{64,96},{80,112},{96,64},{112,80},{1... | collective-permute-start | bytes 1572872 | tf_op jit(solution)/shard_map/gather_blocks/ppermute | solution.py:247
  49.9 3.3 %collective-permute-start.2 = (bf16[16,128,128]{2,1,0:T(8,128)(2,1)}, bf16[16,128,128]{2,1,0:T(8,128)(2,1)}, u32[]{:S(2)}, u32[]{:S(2)}) collective-permute-start(bf16[16,128,128]{2,1,0:T(8,128)(2,1)} %all-to-all-done.refs_3_.refs_5_), channel_id=1, source_target_pairs={{0,48},{16,0},{32,16},{48,32},{64,112},{80,64},{96,80},{112,96},{1... | collective-permute-start | bytes 1572872 | tf_op jit(solution)/shard_map/gather_blocks/ppermute | solution.py:247
  53.3 2.3 %hidden.1 = (bf16[13,128,128]{2,1,0:T(8,128)(2,1)}, bf16[13,128,128]{2,1,0:T(8,128)(2,1)}) custom-call(bf16[128,1664]{1,0:T(8,128)(2,1)} %refs_3_.1, bf16[128,1664]{1,0:T(8,128)(2,1)} %refs_4_.1), custom_call_target="tpu_custom_call" | custom-call | flops 1000000000 | bytes 4000000 | tf_op jit(solution)/shard_map/hidden/pallas_call | solution.py:54
  55.5 0.1 all-gather.2.cloned.1.call-done.refs_3_.refs_2_
  55.6 5.5 %terms.1 = bf16[96,128,128]{2,1,0:T(8,128)(2,1)} custom-call(s32[96]{0:T(128)} %bitcast.9, s32[96]{0:T(128)} %bitcast.12, bf16[13,128,128]{2,1,0:T(8,128)(2,1)} %get-tuple-element.20.refs_2_, bf16[64,128,128]{2,1,0:T(8,128)(2,1)} %all-gather.2.cloned.1.call-done.refs_3_.refs_2_), custom_call_target="tpu_custom_call" | custom-call | flops 1610612736 | bytes 6000000 | tf_op jit(solution)/shard_map/terms/pallas_call | solution.py:54
  61.1 9.9 %all-to-all-done.1.refs_7_.refs_9_ = bf16[32,128,128]{2,1,0:T(8,128)(2,1)S(1)} async-done(((bf16[32,128,128]{2,1,0:T(8,128)(2,1)}), bf16[32,128,128]{2,1,0:T(8,128)(2,1)S(1)}, u32[]{:S(2)}, u32[]{:S(2)}) %all-to-all-start.1) | async-done | bytes 1048608 | tf_op jit(solution)/shard_map/gather_blocks/all_to_all | solution.py:226
  71.0 1.0 copy-done
  72.0 4.3 %all-to-all-start.2 = ((bf16[96,128,128]{2,1,0:T(8,128)(2,1)}), bf16[96,128,128]{2,1,0:T(8,128)(2,1)S(1)}, u32[]{:S(2)}, u32[]{:S(2)}) async-start(bf16[96,128,128]{2,1,0:T(8,128)(2,1)} %terms.1), calls=%async_computation.3 | async-start | bytes 6291456 | tf_op jit(solution)/shard_map/sum_terms_near/all_to_all | solution.py:226
  76.3 0.0 reduce-scatter.2.cloned.1.call-start
  76.4 0.0 collective-permute-done.refs_4_.refs_6_
  76.4 5.2 %forward.1 = (bf16[32,128,128]{2,1,0:T(8,128)(2,1)}, bf16[32,128,128]{2,1,0:T(8,128)(2,1)}) custom-call(s32[96]{0:T(128)} %bitcast.10, s32[96]{0:T(128)} %bitcast.13, bf16[13,128,128]{2,1,0:T(8,128)(2,1)} %get-tuple-element.23.refs_2_, bf16[16,128,128]{2,1,0:T(8,128)(2,1)} %all-to-all-done.refs_3_.refs_5_, ...), custom_call_target="tpu_custom_call" | custom-call | flops 40265318400 | bytes 6000000 | tf_op jit(solution)/shard_map/forward/pallas_call | solution.py:54
  81.6 1.9 %collective-permute-start.3 = (bf16[32,128,128]{2,1,0:T(8,128)(2,1)}, bf16[32,128,128]{2,1,0:T(8,128)(2,1)}, u32[]{:S(2)}, u32[]{:S(2)}) collective-permute-start(bf16[32,128,128]{2,1,0:T(8,128)(2,1)} %get-tuple-element.27), channel_id=1, source_target_pairs={{0,1},{1,0},{2,3},{3,2},{4,5},{5,4},{6,7},{7,6},{8,9},{9,8},{10,11... | collective-permute-start | bytes 3145736 | tf_op jit(solution)/shard_map/sum_output/ppermute | solution.py:269
  83.5 3.0 %collective-permute-done.3.refs_1_ = bf16[32,128,128]{2,1,0:T(8,128)(2,1)} collective-permute-done((bf16[32,128,128]{2,1,0:T(8,128)(2,1)}, bf16[32,128,128]{2,1,0:T(8,128)(2,1)}, u32[]{:S(2)}, u32[]{:S(2)}) %collective-permute-start.3) | collective-permute-done | bytes 1048608 | tf_op jit(solution)/shard_map/sum_output/ppermute | solution.py:269
  86.5 2.4 %sum_output.2 = bf16[32,128,128]{2,1,0:T(8,128)(2,1)} custom-call(bf16[32,128,128]{2,1,0:T(8,128)(2,1)} %get-tuple-element.26.refs_0_, bf16[32,128,128]{2,1,0:T(8,128)(2,1)} %collective-permute-done.3.refs_1_), custom_call_target="tpu_custom_call" | custom-call | bytes 3000000 | tf_op jit(solution)/shard_map/sum_output/pallas_call | solution.py:54
  88.9 0.0 reduce-scatter.2.cloned.1.call-update
  88.9 7.0 %backward.1 = (bf16[128,1664]{1,0:T(8,128)(2,1)}, bf16[128,1664]{1,0:T(8,128)(2,1)}) custom-call(s32[96]{0:T(128)} %bitcast.11, s32[96]{0:T(128)} %bitcast.14, bf16[64,128,128]{2,1,0:T(8,128)(2,1)} %all-gather.2.cloned.1.call-done.refs_3_.refs_2_, bf16[128,1664]{1,0:T(8,128)(2,1)} %refs_3_.1, bf16[128,1664]{1,0:T(8,128)(2,1)} %refs_4_.1, ...), custom_call_target="tpu_custom_call" | custom-call | flops 1610612736 | bytes 8000000 | tf_op jit(solution)/shard_map/backward/pallas_call | solution.py:54
  95.9 17.9 %all-to-all-done.2.refs_0_ = bf16[96,128,128]{2,1,0:T(8,128)(2,1)S(1)} async-done(((bf16[96,128,128]{2,1,0:T(8,128)(2,1)}), bf16[96,128,128]{2,1,0:T(8,128)(2,1)S(1)}, u32[]{:S(2)}, u32[]{:S(2)}) %all-to-all-start.2) | async-done | bytes 3145760 | tf_op jit(solution)/shard_map/sum_terms_near/all_to_all | solution.py:226
  113.8 1.2 sum_terms_apart.2
  114.9 3.5 %all-to-all-start.3 = ((bf16[12,128,128]{2,1,0:T(8,128)(2,1)}), bf16[12,128,128]{2,1,0:T(8,128)(2,1)S(1)}, u32[]{:S(2)}, u32[]{:S(2)}) async-start(bf16[12,128,128]{2,1,0:T(8,128)(2,1)} %sum_terms_apart.2), calls=%async_computation.4 | async-start | bytes 786432 | tf_op jit(solution)/shard_map/sum_terms_apart/all_to_all | solution.py:226
  118.4 7.2 %reduce-scatter.2.cloned.1.call-done.refs_0_ = bf16[4,128,128]{2,1,0:T(8,128)(2,1)} async-done(((bf16[32,128,128]{2,1,0:T(8,128)(2,1)}), bf16[4,128,128]{2,1,0:T(8,128)(2,1)}) %reduce-scatter.2.cloned.1.call-update) | async-done | bytes 131088 | tf_op jit(solution)/shard_map/sum_output/reduce_scatter | solution.py:275
  125.6 1.6 %sum_output.3 = bf16[128,512]{1,0:T(8,128)(2,1)} custom-call(bf16[4,128,128]{2,1,0:T(8,128)(2,1)} %reduce-scatter.2.cloned.1.call-done.refs_0_), custom_call_target="tpu_custom_call" | custom-call | bytes 100000 | tf_op jit(solution)/shard_map/sum_output/pallas_call | solution.py:54
  127.2 4.5 %all-to-all-done.3.refs_0_ = bf16[12,128,128]{2,1,0:T(8,128)(2,1)S(1)} async-done(((bf16[12,128,128]{2,1,0:T(8,128)(2,1)}), bf16[12,128,128]{2,1,0:T(8,128)(2,1)S(1)}, u32[]{:S(2)}, u32[]{:S(2)}) %all-to-all-start.3) | async-done | bytes 393248 | tf_op jit(solution)/shard_map/sum_terms_apart/all_to_all | solution.py:226
  131.8 0.7 sum_terms_apart.3
  (3 shorter events, 0.0 us)
Async XLA Ops:
  7.2 48.4 %all-gather.2.cloned.1.call-start = ((), (), s32[]{:S(2)}) async-start(), calls=%async_computation.5 | async-start | bytes 2228224 | tf_op jit(solution)/shard_map/gather_out_grad/all_gather | solution.py:242
  9.1 27.9 %all-to-all-start = ((bf16[16,128,128]{2,1,0:T(8,128)(2,1)}), bf16[16,128,128]{2,1,0:T(8,128)(2,1)}, u32[]{:S(2)}, u32[]{:S(2)}) async-start(bf16[16,128,128]{2,1,0:T(8,128)(2,1)} %get-tuple-element.24), calls=%async_computation | async-start | bytes 1048576 | tf_op jit(solution)/shard_map/gather_blocks/all_to_all | solution.py:226
  38.3 32.7 %all-to-all-start.1 = ((bf16[32,128,128]{2,1,0:T(8,128)(2,1)}), bf16[32,128,128]{2,1,0:T(8,128)(2,1)S(1)}, u32[]{:S(2)}, u32[]{:S(2)}) async-start(bf16[32,128,128]{2,1,0:T(8,128)(2,1)} %bitcast.3), calls=%async_computation.1 | async-start | bytes 2097152 | tf_op jit(solution)/shard_map/gather_blocks/all_to_all | solution.py:226
  41.9 34.5 %collective-permute-start = (bf16[16,128,128]{2,1,0:T(8,128)(2,1)}, bf16[16,128,128]{2,1,0:T(8,128)(2,1)}, u32[]{:S(2)}, u32[]{:S(2)}) collective-permute-start(bf16[16,128,128]{2,1,0:T(8,128)(2,1)} %all-to-all-done.refs_3_.refs_5_), channel_id=1, source_target_pairs={{0,16},{16,32},{32,48},{48,0},{64,80},{80,96},{96,112},{112,64},{1... | collective-permute-start | bytes 1572872 | tf_op jit(solution)/shard_map/gather_blocks/ppermute | solution.py:247
  45.3 31.1 %collective-permute-start.1 = (bf16[16,128,128]{2,1,0:T(8,128)(2,1)}, bf16[16,128,128]{2,1,0:T(8,128)(2,1)}, u32[]{:S(2)}, u32[]{:S(2)}) collective-permute-start(bf16[16,128,128]{2,1,0:T(8,128)(2,1)} %all-to-all-done.refs_3_.refs_5_), channel_id=1, source_target_pairs={{0,32},{16,48},{32,0},{48,16},{64,96},{80,112},{96,64},{112,80},{1... | collective-permute-start | bytes 1572872 | tf_op jit(solution)/shard_map/gather_blocks/ppermute | solution.py:247
  49.9 26.5 %collective-permute-start.2 = (bf16[16,128,128]{2,1,0:T(8,128)(2,1)}, bf16[16,128,128]{2,1,0:T(8,128)(2,1)}, u32[]{:S(2)}, u32[]{:S(2)}) collective-permute-start(bf16[16,128,128]{2,1,0:T(8,128)(2,1)} %all-to-all-done.refs_3_.refs_5_), channel_id=1, source_target_pairs={{0,48},{16,0},{32,16},{48,32},{64,112},{80,64},{96,80},{112,96},{1... | collective-permute-start | bytes 1572872 | tf_op jit(solution)/shard_map/gather_blocks/ppermute | solution.py:247
  71.0 1.0 copy-start
  72.0 41.8 %all-to-all-start.2 = ((bf16[96,128,128]{2,1,0:T(8,128)(2,1)}), bf16[96,128,128]{2,1,0:T(8,128)(2,1)S(1)}, u32[]{:S(2)}, u32[]{:S(2)}) async-start(bf16[96,128,128]{2,1,0:T(8,128)(2,1)} %terms.1), calls=%async_computation.3 | async-start | bytes 6291456 | tf_op jit(solution)/shard_map/sum_terms_near/all_to_all | solution.py:226
  76.3 49.3 %reduce-scatter.2.cloned.1.call-start = ((), (), s32[]{:S(2)}) async-start(), calls=%async_computation.6 | async-start | bytes 1179648 | tf_op jit(solution)/shard_map/sum_output/reduce_scatter | solution.py:275
  81.6 4.9 %collective-permute-start.3 = (bf16[32,128,128]{2,1,0:T(8,128)(2,1)}, bf16[32,128,128]{2,1,0:T(8,128)(2,1)}, u32[]{:S(2)}, u32[]{:S(2)}) collective-permute-start(bf16[32,128,128]{2,1,0:T(8,128)(2,1)} %get-tuple-element.27), channel_id=1, source_target_pairs={{0,1},{1,0},{2,3},{3,2},{4,5},{5,4},{6,7},{7,6},{8,9},{9,8},{10,11... | collective-permute-start | bytes 3145736 | tf_op jit(solution)/shard_map/sum_output/ppermute | solution.py:269
  114.9 16.8 %all-to-all-start.3 = ((bf16[12,128,128]{2,1,0:T(8,128)(2,1)}), bf16[12,128,128]{2,1,0:T(8,128)(2,1)S(1)}, u32[]{:S(2)}, u32[]{:S(2)}) async-start(bf16[12,128,128]{2,1,0:T(8,128)(2,1)} %sum_terms_apart.2), calls=%async_computation.4 | async-start | bytes 786432 | tf_op jit(solution)/shard_map/sum_terms_apart/all_to_all | solution.py:226
Sparse Core Ops, SparseCore 0:
  10.7 44.8 all-gather.1
  89.0 36.5 reduce-scatter.1

commit v5 on v4

--- a/solution.py
+++ b/solution.py
@@ -78,9 +78,9 @@
     return block_of(i // NX, lax.rem(i, NX), FAR)
 
 
-def each_block(fetch, first, me_x, visit):
+def each_block(fetch, first, near_ref, me_x, visit):
     for a in range(NX + 1):
-        ref = fetch(first + a)
+        ref = fetch(first + a) if a < NX else near_ref
 
         def some(g, carry, a=a, ref=ref):
             entries = [g * STEP + j for j in range(STEP)]
@@ -131,7 +131,7 @@
         leave(g).wait()
 
 
-def forward_kernel(fetch, rows_ref, cols_ref, keep_ref, send_ref, total, keep, send, sems):
+def forward_kernel(fetch, rows_ref, cols_ref, near_ref, keep_ref, send_ref, total, keep, send, sems):
     me_x, core = lax.rem(lax.axis_index("fsdp"), NX), lax.rem(lax.axis_index("tensor"), 2)
     total[...] = jnp.zeros_like(total)
     hid_ref = fetch(0)
@@ -142,7 +142,7 @@
         ]
         for c, value in found:
             total[c] += value
-    each_block(fetch, 1, me_x, visit)
+    each_block(fetch, 1, near_ref, me_x, visit)
 
     def leave(y):
         here = pl.ds(y * 4, 4)
@@ -165,7 +165,7 @@
             copy.wait()
 
 
-def backward_kernel(fetch, rows_ref, cols_ref, d_gate_ref, d_up_ref, total):
+def backward_kernel(fetch, rows_ref, cols_ref, near_ref, d_gate_ref, d_up_ref, total):
     total[...] = jnp.zeros_like(total)
     grad_ref, gate_ref, up_ref = fetch(0), fetch(1), fetch(2)
 
@@ -177,7 +177,7 @@
         ]
         for r, value in found:
             total[r] += value
-    each_block(fetch, 3, lax.rem(lax.axis_index("fsdp"), NX), visit)
+    each_block(fetch, 3, near_ref, lax.rem(lax.axis_index("fsdp"), NX), visit)
     for r in range(HID_TILES):
         here = slice(r * BLK, (r + 1) * BLK)
         gate = gate_ref[:, here].astype(jnp.float32)
@@ -258,7 +258,7 @@
         terms = exchange(terms, NEAR_GROUPS)
     with jax.named_scope("forward"):
         keep, send = call(
-            forward_kernel, (tiles(32), tiles(32)), (rows, cols), (hid, *parts), out_spec=HBM,
+            forward_kernel, (tiles(32), tiles(32)), (rows, cols), (hid, *parts[:NX]), (parts[NX],), out_spec=HBM, vmem=56,
             scratch=[
                 pltpu.VMEM((WIDTH_TILES, BLK, BLK), jnp.float32), pltpu.VMEM((32, BLK, BLK), jnp.bfloat16),
                 pltpu.VMEM((32, BLK, BLK), jnp.bfloat16), pltpu.SemaphoreType.DMA((2, NY)),
@@ -269,7 +269,7 @@
         swapped = lax.ppermute(send, "tensor", CORE_SWAP)
         pair = call(
             pair_kernel, tiles(32), (), (), (keep, swapped), out_spec=HBM, near_spec=HBM,
-            scratch=[*[pltpu.VMEM((32, BLK, BLK), jnp.bfloat16)] * 3, pltpu.SemaphoreType.DMA((3, 4))], moved=3 * 10**6,
+            scratch=[*[pltpu.VMEM((32, BLK, BLK), jnp.bfloat16)] * 3, pltpu.SemaphoreType.DMA((3, 4))], moved=3 * 10**6, vmem=56,
         )
         pair, rows_late = lax.optimization_barrier((pair, rows))
         output = lax.psum_scatter(pair, "tensor", scatter_dimension=0, axis_index_groups=Y_GROUPS, tiled=True)
@@ -277,8 +277,8 @@
     with jax.named_scope("backward"):
         wide = jax.ShapeDtypeStruct(gate_pre.shape, jnp.bfloat16)
         d_gate, d_up = call(
-            backward_kernel, (wide, wide), (rows_late, cols), (grad_tiles, gate_pre, up_pre, *parts),
-            scratch=[pltpu.VMEM((HID_TILES, BLK, BLK), jnp.float32)], flops=8 * macs, moved=8 * 10**6, vmem=60,
+            backward_kernel, (wide, wide), (rows_late, cols), (grad_tiles, gate_pre, up_pre, *parts[:NX]), (parts[NX],),
+            scratch=[pltpu.VMEM((HID_TILES, BLK, BLK), jnp.float32)], flops=8 * macs, moved=8 * 10**6, vmem=56,
         )
     with jax.named_scope("sum_terms_apart"):
         terms, d_gate, d_up = lax.optimization_barrier((terms, d_gate, d_up))

time: 140 us -> 140 us (level)
  waiting for transfers between devices: 47.7 us -> 45.6 us
    all_to_all x4, waiting for transfers between devices: 37.4 us -> 33.8 us  [exchange(): return lax.all_to_all(a, 'fsdp', 0, 0, tiled=True, axis_index_groups=groups)]
    reduce_scatter x1, waiting for transfers between devices: 7.23 us -> 8.75 us  [shards(): lax.psum_scatter(pair, 'tensor', scatter_dimension=0, axis_index_groups=Y...]
  transfers between devices with their start and end apart: 10 -> 10, of which waited for: 7 -> 7; matrix products, arithmetic and copies ran while one was open for 1% -> 1% of each run, Pallas kernels for 18% -> 19%
where the time goes in v5:
time: 140 us; the launch traced here: 139 us
  waiting for transfers between devices  45.6 us (33%)
  starting transfers between devices  35 us (25%)
  Pallas kernels  28.7 us (20%)
  between operations  14.2 us (10%)
  blocking collectives  12.5 us (9%)
  local copies, waits for them, and re-layouts  3.28 us (2%)
    all_to_all x4, waiting for transfers between devices, exchange(): return lax.all_to_all(a, 'fsdp', 0, 0, tiled=True, axis_index_groups=groups)  33.8 us
    pallas_call x9, Pallas kernels, call(): pl.pallas_call(body, out_shape=outs, in_specs=[SMEM] * n + [HBM] * m + [n...  28.7 us
    all_to_all x4, starting transfers between devices, exchange(): return lax.all_to_all(a, 'fsdp', 0, 0, tiled=True, axis_index_groups=groups)  21.7 us
    all_gather x1, blocking collectives, shards(): lax.all_gather(near, 'fsdp', axis=0, axis_index_groups=X_GROUPS, tiled=True)  12.5 us
    ppermute x3, starting transfers between devices, shards(): lax.ppermute(far, 'fsdp', x_shift(s))  11.4 us
    reduce_scatter x1, waiting for transfers between devices, shards(): lax.psum_scatter(pair, 'tensor', scatter_dimension=0, axis_index_groups=Y...  8.75 us
    ppermute x1, waiting for transfers between devices, shards(): swapped = lax.ppermute(send, 'tensor', CORE_SWAP)  2.84 us
  transfers between devices with their start and end apart: 10, of which 7 were waited for; matrix products, arithmetic and copies ran while one was open for 1% of the time, Pallas kernels for 19%

profile of v5, /device:TPU:56, one launch (start us, length us, event | category | flops | bytes accessed | tf_op | source)
XLA Modules:
  0.0 139.3 jit_solution(764115601335968377)
XLA Ops:
  7.2 0.0 all-gather.2.cloned.1.call-start
  7.2 1.9 %gather_out_grad.1 = (bf16[4,128,128]{2,1,0:T(8,128)(2,1)}, bf16[16,128,128]{2,1,0:T(8,128)(2,1)}, bf16[1,128,128]{2,1,0:T(8,128)(2,1)}) custom-call(bf16[128,512]{1,0:T(8,128)(2,1)} %refs_0_.3, bf16[3,128,128]{2,1,0:T(8,128)(2,1)} %bitcast.8), custom_call_target="tpu_custom_call" | custom-call | bytes 1000000 | tf_op jit(solution)/shard_map/gather_out_grad/pallas_call | solution.py:54
  9.1 0.0 all-gather.2.cloned.1.call-update
  9.1 10.3 %all-to-all-start = ((bf16[16,128,128]{2,1,0:T(8,128)(2,1)}), bf16[16,128,128]{2,1,0:T(8,128)(2,1)}, u32[]{:S(2)}, u32[]{:S(2)}) async-start(bf16[16,128,128]{2,1,0:T(8,128)(2,1)} %get-tuple-element.24), calls=%async_computation | async-start | bytes 1048576 | tf_op jit(solution)/shard_map/gather_blocks/all_to_all | solution.py:226
  19.4 12.5 %all_gather.7 = bf16[4,128,128]{2,1,0:T(8,128)(2,1)S(1)} all-gather(bf16[1,128,128]{2,1,0:T(8,128)(2,1)} %get-tuple-element.25), channel_id=1, replica_groups={{0,16,32,48},{64,80,96,112},{128,144,160,176},{192,208,224,240},{256,27..., dimensions={0}, use_global_device_ids=true | all-gather | bytes 163840 | tf_op jit(solution)/shard_map/gather_blocks/all_gather | solution.py:245
  32.0 5.1 %all-to-all-done.refs_3_.refs_5_ = bf16[16,128,128]{2,1,0:T(8,128)(2,1)} async-done(((bf16[16,128,128]{2,1,0:T(8,128)(2,1)}), bf16[16,128,128]{2,1,0:T(8,128)(2,1)}, u32[]{:S(2)}, u32[]{:S(2)}) %all-to-all-start) | async-done | bytes 524320 | tf_op jit(solution)/shard_map/gather_blocks/all_to_all | solution.py:226
  37.0 1.2 broadcast_in_dim.2
  38.3 3.6 %all-to-all-start.1 = ((bf16[32,128,128]{2,1,0:T(8,128)(2,1)}), bf16[32,128,128]{2,1,0:T(8,128)(2,1)S(1)}, u32[]{:S(2)}, u32[]{:S(2)}) async-start(bf16[32,128,128]{2,1,0:T(8,128)(2,1)} %bitcast.3), calls=%async_computation.1 | async-start | bytes 2097152 | tf_op jit(solution)/shard_map/gather_blocks/all_to_all | solution.py:226
  41.8 3.4 %collective-permute-start = (bf16[16,128,128]{2,1,0:T(8,128)(2,1)}, bf16[16,128,128]{2,1,0:T(8,128)(2,1)}, u32[]{:S(2)}, u32[]{:S(2)}) collective-permute-start(bf16[16,128,128]{2,1,0:T(8,128)(2,1)} %all-to-all-done.refs_3_.refs_5_), channel_id=1, source_target_pairs={{0,16},{16,32},{32,48},{48,0},{64,80},{80,96},{96,112},{112,64},{1... | collective-permute-start | bytes 1572872 | tf_op jit(solution)/shard_map/gather_blocks/ppermute | solution.py:247
  45.2 4.6 %collective-permute-start.1 = (bf16[16,128,128]{2,1,0:T(8,128)(2,1)}, bf16[16,128,128]{2,1,0:T(8,128)(2,1)}, u32[]{:S(2)}, u32[]{:S(2)}) collective-permute-start(bf16[16,128,128]{2,1,0:T(8,128)(2,1)} %all-to-all-done.refs_3_.refs_5_), channel_id=1, source_target_pairs={{0,32},{16,48},{32,0},{48,16},{64,96},{80,112},{96,64},{112,80},{1... | collective-permute-start | bytes 1572872 | tf_op jit(solution)/shard_map/gather_blocks/ppermute | solution.py:247
  49.9 3.3 %collective-permute-start.2 = (bf16[16,128,128]{2,1,0:T(8,128)(2,1)}, bf16[16,128,128]{2,1,0:T(8,128)(2,1)}, u32[]{:S(2)}, u32[]{:S(2)}) collective-permute-start(bf16[16,128,128]{2,1,0:T(8,128)(2,1)} %all-to-all-done.refs_3_.refs_5_), channel_id=1, source_target_pairs={{0,48},{16,0},{32,16},{48,32},{64,112},{80,64},{96,80},{112,96},{1... | collective-permute-start | bytes 1572872 | tf_op jit(solution)/shard_map/gather_blocks/ppermute | solution.py:247
  53.2 2.3 %hidden.1 = (bf16[13,128,128]{2,1,0:T(8,128)(2,1)}, bf16[13,128,128]{2,1,0:T(8,128)(2,1)}) custom-call(bf16[128,1664]{1,0:T(8,128)(2,1)} %refs_3_.1, bf16[128,1664]{1,0:T(8,128)(2,1)} %refs_4_.1), custom_call_target="tpu_custom_call" | custom-call | flops 1000000000 | bytes 4000000 | tf_op jit(solution)/shard_map/hidden/pallas_call | solution.py:54
  55.5 0.1 all-gather.2.cloned.1.call-done.refs_3_.refs_2_
  55.6 5.4 %terms.1 = bf16[96,128,128]{2,1,0:T(8,128)(2,1)} custom-call(s32[96]{0:T(128)} %bitcast.9, s32[96]{0:T(128)} %bitcast.12, bf16[13,128,128]{2,1,0:T(8,128)(2,1)} %get-tuple-element.20.refs_2_, bf16[64,128,128]{2,1,0:T(8,128)(2,1)} %all-gather.2.cloned.1.call-done.refs_3_.refs_2_), custom_call_target="tpu_custom_call" | custom-call | flops 1610612736 | bytes 6000000 | tf_op jit(solution)/shard_map/terms/pallas_call | solution.py:54
  61.1 9.9 %all-to-all-done.1.refs_7_.refs_9_ = bf16[32,128,128]{2,1,0:T(8,128)(2,1)S(1)} async-done(((bf16[32,128,128]{2,1,0:T(8,128)(2,1)}), bf16[32,128,128]{2,1,0:T(8,128)(2,1)S(1)}, u32[]{:S(2)}, u32[]{:S(2)}) %all-to-all-start.1) | async-done | bytes 1048608 | tf_op jit(solution)/shard_map/gather_blocks/all_to_all | solution.py:226
  71.0 1.0 copy-done
  72.0 4.3 %all-to-all-start.2 = ((bf16[96,128,128]{2,1,0:T(8,128)(2,1)}), bf16[96,128,128]{2,1,0:T(8,128)(2,1)S(1)}, u32[]{:S(2)}, u32[]{:S(2)}) async-start(bf16[96,128,128]{2,1,0:T(8,128)(2,1)} %terms.1), calls=%async_computation.3 | async-start | bytes 6291456 | tf_op jit(solution)/shard_map/sum_terms_near/all_to_all | solution.py:226
  76.3 0.0 reduce-scatter.2.cloned.1.call-start
  76.3 5.8 %forward.1 = (bf16[32,128,128]{2,1,0:T(8,128)(2,1)}, bf16[32,128,128]{2,1,0:T(8,128)(2,1)}) custom-call(s32[96]{0:T(128)} %bitcast.10, s32[96]{0:T(128)} %bitcast.13, bf16[13,128,128]{2,1,0:T(8,128)(2,1)} %get-tuple-element.23.refs_2_, bf16[16,128,128]{2,1,0:T(8,128)(2,1)} %all-to-all-done.refs_3_.refs_5_, ...), custom_call_target="tpu_custom_call" | custom-call | flops 40265318400 | bytes 6000000 | tf_op jit(solution)/shard_map/forward/pallas_call | solution.py:54
  82.1 1.9 %collective-permute-start.3 = (bf16[32,128,128]{2,1,0:T(8,128)(2,1)}, bf16[32,128,128]{2,1,0:T(8,128)(2,1)S(1)}, u32[]{:S(2)}, u32[]{:S(2)}) collective-permute-start(bf16[32,128,128]{2,1,0:T(8,128)(2,1)} %get-tuple-element.27), channel_id=1, source_target_pairs={{0,1},{1,0},{2,3},{3,2},{4,5},{5,4},{6,7},{7,6},{8,9},{9,8},{10,11... | collective-permute-start | bytes 3145736 | tf_op jit(solution)/shard_map/sum_output/ppermute | solution.py:269
  84.1 2.8 %collective-permute-done.3.refs_1_ = bf16[32,128,128]{2,1,0:T(8,128)(2,1)S(1)} collective-permute-done((bf16[32,128,128]{2,1,0:T(8,128)(2,1)}, bf16[32,128,128]{2,1,0:T(8,128)(2,1)S(1)}, u32[]{:S(2)}, u32[]{:S(2)}) %collective-permute-start.3) | collective-permute-done | bytes 1048608 | tf_op jit(solution)/shard_map/sum_output/ppermute | solution.py:269
  86.9 1.1 copy-done.1
  88.0 2.4 %sum_output.2 = bf16[32,128,128]{2,1,0:T(8,128)(2,1)} custom-call(bf16[32,128,128]{2,1,0:T(8,128)(2,1)} %get-tuple-element.26.refs_0_, bf16[32,128,128]{2,1,0:T(8,128)(2,1)} %copy-done.1), custom_call_target="tpu_custom_call" | custom-call | bytes 3000000 | tf_op jit(solution)/shard_map/sum_output/pallas_call | solution.py:54
  90.3 0.0 reduce-scatter.2.cloned.1.call-update
  90.4 7.5 %backward.1 = (bf16[128,1664]{1,0:T(8,128)(2,1)}, bf16[128,1664]{1,0:T(8,128)(2,1)}) custom-call(s32[96]{0:T(128)} %bitcast.11, s32[96]{0:T(128)} %bitcast.14, bf16[64,128,128]{2,1,0:T(8,128)(2,1)} %all-gather.2.cloned.1.call-done.refs_3_.refs_2_, bf16[128,1664]{1,0:T(8,128)(2,1)} %refs_3_.1, bf16[128,1664]{1,0:T(8,128)(2,1)} %refs_4_.1, ...), custom_call_target="tpu_custom_call" | custom-call | flops 1610612736 | bytes 8000000 | tf_op jit(solution)/shard_map/backward/pallas_call | solution.py:54
  97.9 15.9 %all-to-all-done.2.refs_0_ = bf16[96,128,128]{2,1,0:T(8,128)(2,1)S(1)} async-done(((bf16[96,128,128]{2,1,0:T(8,128)(2,1)}), bf16[96,128,128]{2,1,0:T(8,128)(2,1)S(1)}, u32[]{:S(2)}, u32[]{:S(2)}) %all-to-all-start.2) | async-done | bytes 3145760 | tf_op jit(solution)/shard_map/sum_terms_near/all_to_all | solution.py:226
  113.7 1.2 sum_terms_apart.2
  114.9 3.5 %all-to-all-start.3 = ((bf16[12,128,128]{2,1,0:T(8,128)(2,1)}), bf16[12,128,128]{2,1,0:T(8,128)(2,1)S(1)}, u32[]{:S(2)}, u32[]{:S(2)}) async-start(bf16[12,128,128]{2,1,0:T(8,128)(2,1)} %sum_terms_apart.2), calls=%async_computation.4 | async-start | bytes 786432 | tf_op jit(solution)/shard_map/sum_terms_apart/all_to_all | solution.py:226
  118.4 8.7 %reduce-scatter.2.cloned.1.call-done.refs_0_ = bf16[4,128,128]{2,1,0:T(8,128)(2,1)} async-done(((bf16[32,128,128]{2,1,0:T(8,128)(2,1)}), bf16[4,128,128]{2,1,0:T(8,128)(2,1)}) %reduce-scatter.2.cloned.1.call-update) | async-done | bytes 131088 | tf_op jit(solution)/shard_map/sum_output/reduce_scatter | solution.py:275
  127.1 1.6 %sum_output.3 = bf16[128,512]{1,0:T(8,128)(2,1)} custom-call(bf16[4,128,128]{2,1,0:T(8,128)(2,1)} %reduce-scatter.2.cloned.1.call-done.refs_0_), custom_call_target="tpu_custom_call" | custom-call | bytes 100000 | tf_op jit(solution)/shard_map/sum_output/pallas_call | solution.py:54
  128.7 3.0 %all-to-all-done.3.refs_0_ = bf16[12,128,128]{2,1,0:T(8,128)(2,1)S(1)} async-done(((bf16[12,128,128]{2,1,0:T(8,128)(2,1)}), bf16[12,128,128]{2,1,0:T(8,128)(2,1)S(1)}, u32[]{:S(2)}, u32[]{:S(2)}) %all-to-all-start.3) | async-done | bytes 393248 | tf_op jit(solution)/shard_map/sum_terms_apart/all_to_all | solution.py:226
  131.7 0.7 sum_terms_apart.3
  (5 shorter events, 0.0 us)
Async XLA Ops:
  7.2 48.4 %all-gather.2.cloned.1.call-start = ((), (), s32[]{:S(2)}) async-start(), calls=%async_computation.5 | async-start | bytes 2228224 | tf_op jit(solution)/shard_map/gather_out_grad/all_gather | solution.py:242
  9.1 27.9 %all-to-all-start = ((bf16[16,128,128]{2,1,0:T(8,128)(2,1)}), bf16[16,128,128]{2,1,0:T(8,128)(2,1)}, u32[]{:S(2)}, u32[]{:S(2)}) async-start(bf16[16,128,128]{2,1,0:T(8,128)(2,1)} %get-tuple-element.24), calls=%async_computation | async-start | bytes 1048576 | tf_op jit(solution)/shard_map/gather_blocks/all_to_all | solution.py:226
  38.3 32.7 %all-to-all-start.1 = ((bf16[32,128,128]{2,1,0:T(8,128)(2,1)}), bf16[32,128,128]{2,1,0:T(8,128)(2,1)S(1)}, u32[]{:S(2)}, u32[]{:S(2)}) async-start(bf16[32,128,128]{2,1,0:T(8,128)(2,1)} %bitcast.3), calls=%async_computation.1 | async-start | bytes 2097152 | tf_op jit(solution)/shard_map/gather_blocks/all_to_all | solution.py:226
  41.8 34.5 %collective-permute-start = (bf16[16,128,128]{2,1,0:T(8,128)(2,1)}, bf16[16,128,128]{2,1,0:T(8,128)(2,1)}, u32[]{:S(2)}, u32[]{:S(2)}) collective-permute-start(bf16[16,128,128]{2,1,0:T(8,128)(2,1)} %all-to-all-done.refs_3_.refs_5_), channel_id=1, source_target_pairs={{0,16},{16,32},{32,48},{48,0},{64,80},{80,96},{96,112},{112,64},{1... | collective-permute-start | bytes 1572872 | tf_op jit(solution)/shard_map/gather_blocks/ppermute | solution.py:247
  45.2 31.1 %collective-permute-start.1 = (bf16[16,128,128]{2,1,0:T(8,128)(2,1)}, bf16[16,128,128]{2,1,0:T(8,128)(2,1)}, u32[]{:S(2)}, u32[]{:S(2)}) collective-permute-start(bf16[16,128,128]{2,1,0:T(8,128)(2,1)} %all-to-all-done.refs_3_.refs_5_), channel_id=1, source_target_pairs={{0,32},{16,48},{32,0},{48,16},{64,96},{80,112},{96,64},{112,80},{1... | collective-permute-start | bytes 1572872 | tf_op jit(solution)/shard_map/gather_blocks/ppermute | solution.py:247
  49.9 26.5 %collective-permute-start.2 = (bf16[16,128,128]{2,1,0:T(8,128)(2,1)}, bf16[16,128,128]{2,1,0:T(8,128)(2,1)}, u32[]{:S(2)}, u32[]{:S(2)}) collective-permute-start(bf16[16,128,128]{2,1,0:T(8,128)(2,1)} %all-to-all-done.refs_3_.refs_5_), channel_id=1, source_target_pairs={{0,48},{16,0},{32,16},{48,32},{64,112},{80,64},{96,80},{112,96},{1... | collective-permute-start | bytes 1572872 | tf_op jit(solution)/shard_map/gather_blocks/ppermute | solution.py:247
  71.0 1.0 copy-start
  72.0 41.8 %all-to-all-start.2 = ((bf16[96,128,128]{2,1,0:T(8,128)(2,1)}), bf16[96,128,128]{2,1,0:T(8,128)(2,1)S(1)}, u32[]{:S(2)}, u32[]{:S(2)}) async-start(bf16[96,128,128]{2,1,0:T(8,128)(2,1)} %terms.1), calls=%async_computation.3 | async-start | bytes 6291456 | tf_op jit(solution)/shard_map/sum_terms_near/all_to_all | solution.py:226
  76.3 50.8 %reduce-scatter.2.cloned.1.call-start = ((), (), s32[]{:S(2)}) async-start(), calls=%async_computation.6 | async-start | bytes 1179648 | tf_op jit(solution)/shard_map/sum_output/reduce_scatter | solution.py:275
  82.1 4.8 %collective-permute-start.3 = (bf16[32,128,128]{2,1,0:T(8,128)(2,1)}, bf16[32,128,128]{2,1,0:T(8,128)(2,1)S(1)}, u32[]{:S(2)}, u32[]{:S(2)}) collective-permute-start(bf16[32,128,128]{2,1,0:T(8,128)(2,1)} %get-tuple-element.27), channel_id=1, source_target_pairs={{0,1},{1,0},{2,3},{3,2},{4,5},{5,4},{6,7},{7,6},{8,9},{9,8},{10,11... | collective-permute-start | bytes 3145736 | tf_op jit(solution)/shard_map/sum_output/ppermute | solution.py:269
  86.9 1.1 copy-start.1
  114.9 16.8 %all-to-all-start.3 = ((bf16[12,128,128]{2,1,0:T(8,128)(2,1)}), bf16[12,128,128]{2,1,0:T(8,128)(2,1)S(1)}, u32[]{:S(2)}, u32[]{:S(2)}) async-start(bf16[12,128,128]{2,1,0:T(8,128)(2,1)} %sum_terms_apart.2), calls=%async_computation.4 | async-start | bytes 786432 | tf_op jit(solution)/shard_map/sum_terms_apart/all_to_all | solution.py:226
Sparse Core Ops, SparseCore 0:
  10.7 44.8 all-gather.1
  90.5 36.5 reduce-scatter.1
